TPU v7x, 256 devices: a whole 4x4x8 slice. The times are simulated.
256 devices in a mesh: pq: 16 (over z_hi, x), rs: 16 (over y, z_lo, core).
Axes of the slice: x: 4, y: 4, z: 8 (z_hi: 4, z_lo: 2; z = z_hi * 2 + z_lo), core: 2. Of those that a mesh axis runs over, the one named last changes fastest.
Arguments:
- integrals: bfloat16 [2, 8192, 65536], P(None, 'pq', 'rs'), may hold values from -6 to 6
- screen: int32 [2, 64, 512], P(None, 'pq', 'rs'), may hold values 0 or 1
- rs_coeff: bfloat16 [65536, 1024], P('rs', 'pq'), may hold values from -0.0234375 to 0.0234375
- pq_coeff: bfloat16 [2, 8192, 1024], P(None, 'pq'), may hold values from -0.0625 to 0.0625
Outputs:
- ovov: float32 [2, 1024, 1024], P(None, 'pq', 'rs')
Inputs may be any that keep to these rules, and one draw needn't show every extreme that they name: `screen`: 1 where a tile survives screening, 0 where it is dropped.
All inputs are finite; a program needn't handle non-finite values. No bound on the sum of `screen` on one device may be relied on, other than what follows from the above.
Results may differ from a plain program's by a relative error of at most 0.0029.
Values may be sent and summed in bfloat16 or wider, within the bound.
No kernel may reach another device: no remote copies, remote signals or barrier semaphores. Data moves between devices by JAX's collectives and lax.ppermute only.
A program may use at most 128 MiB of HBM per device.

v0:
```python
import jax
import jax.numpy as jnp
from jax import lax
from jax.sharding import PartitionSpec as P

TILE = 128


def body(integrals, screen, rs_coeff, pq_coeff):
    slab_count, pq_rows, rs_cols = integrals.shape
    tile_rows = pq_rows // TILE
    tile_cols = rs_cols // TILE
    flags = screen.astype(jnp.bfloat16)
    shaped = integrals.reshape(slab_count, tile_rows, TILE, tile_cols, TILE)
    masked = (shaped * flags[:, :, None, :, None]).reshape(slab_count, pq_rows, rs_cols)
    gathered = lax.all_gather(rs_coeff, "pq", axis=1, tiled=True)
    partial_value = jnp.einsum("spr,ro->spo", masked, gathered, preferred_element_type=jnp.float32)
    half = lax.psum_scatter(partial_value, "rs", scatter_dimension=2, tiled=True).astype(
        jnp.bfloat16
    )
    results = []
    for index_slab in range(slab_count):
        coeff_slab = pq_coeff[index_slab]
        half_slab = half[index_slab]
        results.append(
            lax.psum_scatter(
                jnp.dot(coeff_slab.T, half_slab, preferred_element_type=jnp.float32),
                "pq",
                scatter_dimension=0,
                tiled=True,
            )
        )
    return jnp.stack(results)


def solution(mesh):
    return jax.shard_map(
        body,
        mesh=mesh,
        in_specs=(P(None, "pq", "rs"), P(None, "pq", "rs"), P("rs", "pq"), P(None, "pq", None)),
        out_specs=P(None, "pq", "rs"),
        check_vma=False,
    )
```

profile of v0, /device:TPU:16, one launch (start us, length us, event | category | flops | bytes accessed | tf_op | source)
XLA Modules:
  0.0 399.1 jit_solution(12539710324255346491)
XLA Ops:
  6.5 0.7 all-gather.2.cloned.1.call-update
  7.3 0.0 reduce-scatter.8.cloned.1.call-start
  7.3 0.7 convert_element_type.6
  8.0 4.4 %mul.11 = bf16[2,4,128,32,128]{4,3,2,1,0:T(8,128)(2,1)} broadcast(bf16[2,4,32]{2,1,0:T(4,128)(2,1)S(1)} %convert_element_type.6), dimensions={0,1,3} | broadcast | bytes 8389120 | tf_op jit(solution)/shard_map/mul | solution.py:15
  12.4 13.3 %mul.12 = bf16[2,512,4096]{2,1,0:T(8,128)(2,1)} reshape(bf16[2,4,128,32,128]{4,3,2,1,0:T(8,128)(2,1)} %mul.11) | data formatting | bytes 16777216 | tf_op jit(solution)/shard_map/mul | solution.py:15
  25.7 94.0 %all-gather.2.cloned.1.call-done = bf16[4096,1024]{0,1:T(8,128)(2,1)} async-done(((bf16[4096,64]{0,1:T(8,128)(2,1)}), bf16[4096,1024]{0,1:T(8,128)(2,1)}) %all-gather.2.cloned.1.call-update) | async-done | bytes 8388624 | tf_op jit(solution)/shard_map/all_gather | solution.py:16
  119.7 16.3 %fusion = f32[2,512,1024]{1,2,0:T(8,128)} fusion(bf16[4096,1024]{0,1:T(8,128)(2,1)} %all-gather.2.cloned.1.call-done, bf16[2,512,4096]{2,1,0:T(8,128)(2,1)} %param.4, bf16[2,512,4096]{2,1,0:T(8,128)(2,1)} %mul.12), kind=kOutput, calls=%fused_computation | convolution fusion | flops 8594128896 | bytes 29360128 | tf_op jit(solution)/shard_map/spr,ro->spo/dot_general | solution.py:17
  136.0 0.0 reduce-scatter.8.cloned.1.call-update
  136.1 0.0 reduce-scatter.10.cloned.1.call-start
  136.1 71.0 %reduce-scatter.8.cloned.1.call-done = f32[2,512,64]{1,2,0:T(8,128)} async-done(((f32[2,512,1024]{1,2,0:T(8,128)}), f32[2,512,64]{1,2,0:T(8,128)}) %reduce-scatter.8.cloned.1.call-update) | async-done | bytes 262160 | tf_op jit(solution)/shard_map/reduce_scatter | solution.py:18
  207.1 1.0 convert_element_type.7
  208.0 0.0 copy-done
  208.1 0.3 convolution_bitcast_fusion.1
  208.4 1.0 copy.7
  209.4 0.0 reduce-scatter.10.cloned.1.call-update
  209.4 0.0 reduce-scatter.12.cloned.1.call-start
  209.4 0.3 convolution_bitcast_fusion
  209.7 1.0 copy.9
  210.7 0.0 reduce-scatter.12.cloned.1.call-update
  210.8 93.2 %reduce-scatter.10.cloned.1.call-done = f32[64,64]{1,0:T(8,128)} async-done(((f32[1024,64]{1,0:T(8,128)}), f32[64,64]{1,0:T(8,128)}) %reduce-scatter.10.cloned.1.call-update) | async-done | bytes 16400
  304.0 0.8 copy.8
  304.8 86.2 %reduce-scatter.12.cloned.1.call-done = f32[64,64]{1,0:T(8,128)} async-done(((f32[1024,64]{1,0:T(8,128)}), f32[64,64]{1,0:T(8,128)}) %reduce-scatter.12.cloned.1.call-update) | async-done | bytes 16400
  391.0 0.8 copy.10
  391.9 0.7 copy.6
  (3 shorter events, 0.0 us)
Async XLA Ops:
  6.5 113.2 %all-gather.2.cloned.1.call-start = ((), (), s32[]{:S(2)}) async-start(), calls=%async_computation.3 | async-start | bytes 8912896 | tf_op jit(solution)/shard_map/all_gather | solution.py:16
  7.3 199.8 %reduce-scatter.8.cloned.1.call-start = ((), (), s32[]{:S(2)}) async-start(), calls=%async_computation.4 | async-start | bytes 4456448 | tf_op jit(solution)/shard_map/reduce_scatter | solution.py:18
  25.7 182.3 %copy-start = (bf16[2,512,1024]{2,1,0:T(8,128)(2,1)S(1)}, bf16[2,512,1024]{2,1,0:T(8,128)(2,1)}, u32[]{:S(2)}) copy-start(bf16[2,512,1024]{2,1,0:T(8,128)(2,1)} %param.7) | copy-start | bytes 6291460
  136.1 167.9 %reduce-scatter.10.cloned.1.call-start = ((), (), s32[]{:S(2)}) async-start(), calls=%async_computation.5 | async-start | bytes 557056
  209.4 181.6 %reduce-scatter.12.cloned.1.call-start = ((), (), s32[]{:S(2)}) async-start(), calls=%async_computation.6 | async-start | bytes 557056
Sparse Core Ops, SparseCore 0:
  9.8 109.8 all-gather.1
  136.2 70.8 reduce-scatter.7
  210.6 93.3 reduce-scatter.9
  307.7 83.2 reduce-scatter.11
where the time goes:
time: 400 us; the launch traced here: 399 us
  waiting for transfers between devices  345 us (86%)
  local copies, waits for them, and re-layouts  22.1 us (6%)
  matrix products  16.9 us (4%)
  between operations  13.2 us (3%)
    unnamed x6, waiting for transfers between devices  180 us
    all_gather x1, waiting for transfers between devices, body(): gathered = lax.all_gather(rs_coeff, 'pq', axis=1, tiled=True)  94 us
    reduce_scatter x1, waiting for transfers between devices, body(): lax.psum_scatter(partial_value, 'rs', scatter_dimension=2, tiled=True)  71 us
    mul x2, local copies, waits for them, and re-layouts, body(): shaped * flags[:, :, None, :, None]  17.7 us
    dot_general x1, matrix products, body(): jnp.einsum('spr,ro->spo', masked, gathered, preferred_element_type=jnp.fl...  16.3 us
  transfers between devices with their start and end apart: 4, of which 4 were waited for; matrix products, arithmetic and copies ran while one was open for 5% of the time, Pallas kernels for 0%

commit v1 on v0

v1 whole, which is shorter than its diff:
```python
import functools

import jax
import jax.numpy as jnp
from jax import lax
from jax.experimental import pallas as pl
from jax.experimental.pallas import tpu as pltpu
from jax.sharding import PartitionSpec as P

TILE = 128
F32 = jnp.float32
BF16 = jnp.bfloat16
VMEM_LIMIT = 40 * 1024 * 1024


def pq_shift(value, dz, dx):
    perm = []
    for index in range(16):
        z, x = divmod(index, 4)
        perm.append((index, (z + dz) % 4 * 4 + (x + dx) % 4))
    return lax.ppermute(value, "pq", perm)


def core_swap(value):
    return lax.ppermute(value, "rs", [(index, index ^ 1) for index in range(16)])


def params():
    return pltpu.CompilerParams(vmem_limit_bytes=VMEM_LIMIT)


def cost(flops, bytes_accessed):
    return pl.CostEstimate(flops=flops, bytes_accessed=bytes_accessed, transcendentals=0)


def mask_kernel(screen_ref, a_ref, out_ref):
    row = pl.program_id(0)
    for col in range(a_ref.shape[1] // TILE):
        flag = screen_ref[row, col].astype(F32)
        at = slice(col * TILE, (col + 1) * TILE)
        out_ref[:, at] = (a_ref[:, at].astype(F32) * flag).astype(BF16)


def mask(integrals, screen):
    rows, cols = integrals.shape
    return pl.pallas_call(
        mask_kernel,
        out_shape=jax.ShapeDtypeStruct((rows, cols), BF16),
        grid_spec=pltpu.PrefetchScalarGridSpec(
            num_scalar_prefetch=1,
            grid=(rows // TILE,),
            in_specs=[pl.BlockSpec((TILE, cols), lambda row, _: (row, 0))],
            out_specs=pl.BlockSpec((TILE, cols), lambda row, _: (row, 0)),
        ),
        compiler_params=params(),
        cost_estimate=cost(rows * cols, 4 * rows * cols),
    )(screen, integrals)


def half_kernel(counts, swap_ref, a_ref, *refs):
    pieces, (keep_ref, send_ref) = refs[:-2], refs[-2:]
    a = a_ref[...]

    def product(some):
        value = jnp.concatenate([ref[...] for ref in some], axis=0)
        return lax.dot_general(value, a, (((1,), (1,)), ((), ())), preferred_element_type=F32)

    even = product(pieces[: counts[0]])
    odd = product(pieces[counts[0] :])
    swap = swap_ref[0] != 0
    keep_ref[...] = jnp.where(swap, odd, even)
    send_ref[...] = jnp.where(swap, even, odd)


def half_transform(swap, masked, even, odd):
    rows, cols = masked.shape
    width = 256
    n = sum(piece.shape[0] for piece in even)
    pieces = list(even) + list(odd)
    out = jax.ShapeDtypeStruct((n, rows), F32)
    return pl.pallas_call(
        functools.partial(half_kernel, (len(even), len(odd))),
        out_shape=[out, out],
        grid_spec=pltpu.PrefetchScalarGridSpec(
            num_scalar_prefetch=1,
            grid=(rows // width,),
            in_specs=[pl.BlockSpec((width, cols), lambda at, _: (at, 0))]
            + [pl.BlockSpec(piece.shape, lambda at, _: (0, 0)) for piece in pieces],
            out_specs=[pl.BlockSpec((n, width), lambda at, _: (0, at))] * 2,
        ),
        compiler_params=params(),
        cost_estimate=cost(4 * n * rows * cols, 2 * rows * cols + 4 * n * cols + 8 * n * rows),
    )(swap, masked, *pieces)


def pack_kernel(dest_ref, *refs):
    out_ref = refs[-1]
    slot = 0
    for at in range(0, len(refs) - 1, 2):
        keep_ref, got_ref = refs[at], refs[at + 1]
        for first in range(0, keep_ref.shape[0], 64):
            rows = slice(first, first + 64)
            out_ref[dest_ref[slot]] = (keep_ref[rows, :] + got_ref[rows, :]).astype(BF16)
            slot += 1


def pack(dest, pairs):
    flat = [value for pair in pairs for value in pair]
    rows = flat[0].shape[1]
    return pl.pallas_call(
        pack_kernel,
        out_shape=jax.ShapeDtypeStruct((8, 64, rows), BF16),
        in_specs=[pl.BlockSpec(memory_space=pltpu.SMEM)]
        + [pl.BlockSpec(memory_space=pltpu.VMEM)] * len(flat),
        out_specs=pl.BlockSpec(memory_space=pltpu.VMEM),
        compiler_params=params(),
        cost_estimate=cost(8 * 64 * rows, 10 * 8 * 64 * rows),
    )(dest, *flat)


def second_kernel(x_ref, got_ref, coeff_ref, *refs):
    outs, turned_ref = refs[:-1], refs[-1]
    half = got_ref[0].astype(F32)
    for at in range(1, 8):
        half = half + got_ref[at].astype(F32)
    high = half.astype(BF16)
    low = (half - high.astype(F32)).astype(BF16)
    parts = []
    for slab in range(2):
        at = slice(slab * 512, (slab + 1) * 512)
        coeff = coeff_ref[slab]
        both = jnp.concatenate([high[:, at], low[:, at]], axis=0)
        product = jnp.dot(both, coeff, preferred_element_type=F32)
        parts.append(product[:64] + product[64:])
    turned_ref[...] = jnp.concatenate(parts, axis=0).T
    for dx in range(4):
        x = lax.rem(x_ref[0] + dx, 4)
        for z in range(4):
            first = pl.multiple_of((z * 4 + x) * 64, 64)
            outs[dx][z] = turned_ref[pl.ds(first, 64), :]


def second_transform(x, got, pq_coeff):
    out = jax.ShapeDtypeStruct((4, 64, 128), F32)
    return pl.pallas_call(
        second_kernel,
        out_shape=[out] * 4,
        in_specs=[pl.BlockSpec(memory_space=pltpu.SMEM)]
        + [pl.BlockSpec(memory_space=pltpu.VMEM)] * 2,
        out_specs=[pl.BlockSpec(memory_space=pltpu.VMEM)] * 4,
        scratch_shapes=[pltpu.VMEM((1024, 128), F32)],
        compiler_params=params(),
        cost_estimate=cost(8 * 64 * 512 * 1024, 4 * 1024 * 1024),
    )(x, got, pq_coeff)


def turn_kernel(z_ref, a_ref, b_ref, c_ref, d_ref, *outs):
    for dz in range(4):
        z = lax.rem(z_ref[0] + dz, 4)
        outs[dz][...] = (a_ref[z] + b_ref[z]) + (c_ref[z] + d_ref[z])


def turn(z, parts):
    out = jax.ShapeDtypeStruct((64, 128), F32)
    return pl.pallas_call(
        turn_kernel,
        out_shape=[out] * 4,
        in_specs=[pl.BlockSpec(memory_space=pltpu.SMEM)]
        + [pl.BlockSpec(memory_space=pltpu.VMEM)] * 4,
        out_specs=[pl.BlockSpec(memory_space=pltpu.VMEM)] * 4,
        compiler_params=params(),
        cost_estimate=cost(4 * 64 * 128 * 4, 4 * 64 * 128 * 4 * 5),
    )(z, *parts)


def last_kernel(a_ref, b_ref, c_ref, d_ref, out_ref):
    total = (a_ref[...] + b_ref[...]) + (c_ref[...] + d_ref[...])
    out_ref[0] = total[:, :64]
    out_ref[1] = total[:, 64:]


def last(parts):
    return pl.pallas_call(
        last_kernel,
        out_shape=jax.ShapeDtypeStruct((2, 64, 64), F32),
        in_specs=[pl.BlockSpec(memory_space=pltpu.VMEM)] * 4,
        out_specs=pl.BlockSpec(memory_space=pltpu.VMEM),
        compiler_params=params(),
    )(*parts)


def body(integrals, screen, rs_coeff, pq_coeff):
    slabs, pq_rows, rs_cols = integrals.shape
    pq_at, rs_at = lax.axis_index("pq"), lax.axis_index("rs")
    z, x = pq_at // 4, pq_at % 4
    core = rs_at % 2
    swap = (x + core) % 2

    own = rs_coeff.T
    top, low = slice(0, 32), slice(32, 64)

    z_less = pq_shift(own, 1, 0)
    z_more = pq_shift(own, -1, 0)
    x_less = pq_shift(own, 0, 1)
    x_more = pq_shift(own, 0, -1)
    masked = mask(
        integrals.reshape(slabs * pq_rows, rs_cols),
        screen.reshape(slabs * (pq_rows // TILE), rs_cols // TILE),
    )
    x_two = jnp.concatenate(
        [pq_shift(x_less[top], 0, 1), pq_shift(x_more[low], 0, -1)], axis=0
    )
    z_two = jnp.concatenate(
        [pq_shift(z_less[top], 1, 0), pq_shift(z_more[low], -1, 0)], axis=0
    )
    more_less = pq_shift(z_more, 0, 1)
    more_more = pq_shift(z_more, 0, -1)
    less_two = pq_shift(x_two, 1, 0)
    more_two = pq_shift(x_two, -1, 0)
    two_less = pq_shift(z_two, 0, 1)
    two_more = pq_shift(z_two, 0, -1)
    less_less = pq_shift(z_less, 0, 1)
    less_more = pq_shift(z_less, 0, -1)
    two_two_top = pq_shift(two_less[top], 0, 1)
    two_two_low = pq_shift(two_more[low], 0, -1)

    groups = [
        ([own, x_two], [x_less, x_more], [(0, 0), (0, 2)], [(0, -1), (0, 1)]),
        ([z_less, z_more], [more_less, more_more], [(-1, 0), (1, 0)], [(1, -1), (1, 1)]),
        ([z_two], [two_less], [(2, 0)], [(2, -1)]),
        (
            [less_two, more_two, two_two_top, two_two_low],
            [two_more, less_less, less_more],
            [(-1, 2), (1, 2), (2, 2)],
            [(2, 1), (-1, -1), (-1, 1)],
        ),
    ]
    swap_at = swap.astype(jnp.int32).reshape(1)
    pairs, dest = [], []
    for even, odd, even_at, odd_at in groups:
        keep, send = half_transform(swap_at, masked, even, odd)
        pairs.append((keep, core_swap(send)))
        for (ez, ex), (oz, ox) in zip(even_at, odd_at):
            dz, dx = jnp.where(swap == 0, ez, oz), jnp.where(swap == 0, ex, ox)
            dest.append((z + dz + 4) % 4 * 2 + (x + dx + 4) % 4 // 2)
    packed = pack(jnp.stack(dest).astype(jnp.int32), pairs)
    got = lax.all_to_all(
        packed,
        "rs",
        0,
        0,
        tiled=True,
        axis_index_groups=[[index * 2 + at for index in range(8)] for at in range(2)],
    )
    parts = second_transform(x.astype(jnp.int32).reshape(1), got, pq_coeff)
    parts = [parts[0]] + [pq_shift(parts[dx], 0, dx) for dx in (1, 2, 3)]
    parts = turn(z.astype(jnp.int32).reshape(1), parts)
    parts = [parts[0]] + [pq_shift(parts[dz], dz, 0) for dz in (1, 2, 3)]
    return last(parts)


def solution(mesh):
    return jax.shard_map(
        body,
        mesh=mesh,
        in_specs=(P(None, "pq", "rs"), P(None, "pq", "rs"), P("rs", "pq"), P(None, "pq", None)),
        out_specs=P(None, "pq", "rs"),
        check_vma=False,
    )
```

time: 400 us -> 167 us (0.42)
  waiting for transfers between devices: 345 us -> 43.4 us
  starting transfers between devices: 0.12 us -> 52.8 us
  Pallas kernels: 0 us -> 40.7 us
  blocking collectives: 0 us -> 18.3 us
  matrix products: 16.9 us -> 0 us
  between operations: 13.2 us -> 0.24 us
  local copies, waits for them, and re-layouts: 22.1 us -> 9.56 us
    unnamed x6 -> x0, waiting for transfers between devices: 180 us -> none
    all_gather x1 -> x0, waiting for transfers between devices: 94 us -> none  [body(): gathered = lax.all_gather(rs_coeff, 'pq', axis=1, tiled=True)]
    reduce_scatter x1 -> x0, waiting for transfers between devices: 71 us -> none  [body(): lax.psum_scatter(partial_value, 'rs', scatter_dimension=2, tiled=True)]
    ppermute x0 -> x28, starting transfers between devices: none -> 52.8 us  [the longest x24 52 us: pq_shift(): return lax.ppermute(value, 'pq', perm)]
    ppermute x0 -> x28, waiting for transfers between devices: none -> 43.4 us  [the longest x24 42 us: pq_shift(): return lax.ppermute(value, 'pq', perm)]
    pallas_call x0 -> x9, Pallas kernels: none -> 40.7 us  [the longest x4 30.2 us: half_transform(): pl.pallas_call(functools.partial(half_kernel, (len(even), len(odd))), out...]
    all_to_all x0 -> x1, blocking collectives: none -> 18.3 us  [body(): lax.all_to_all(packed, 'rs', 0, 0, tiled=True, axis_index_groups=[[index...]
    mul x2 -> x0, local copies, waits for them, and re-layouts: 17.7 us -> none  [body(): shaped * flags[:, :, None, :, None]]
  transfers between devices with their start and end apart: 4 -> 28, of which waited for: 4 -> 11; matrix products, arithmetic and copies ran while one was open for 5% -> 2% of each run, Pallas kernels for 0% -> 23%
where the time goes in v1:
time: 167 us; the launch traced here: 165 us
  starting transfers between devices  52.8 us (32%)
  waiting for transfers between devices  43.4 us (26%)
  Pallas kernels  40.7 us (24%)
  blocking collectives  18.3 us (11%)
  local copies, waits for them, and re-layouts  9.56 us (6%)
    ppermute x24, starting transfers between devices, pq_shift(): return lax.ppermute(value, 'pq', perm)  52 us
    ppermute x24, waiting for transfers between devices, pq_shift(): return lax.ppermute(value, 'pq', perm)  42 us
    pallas_call x4, Pallas kernels, half_transform(): pl.pallas_call(functools.partial(half_kernel, (len(even), len(odd))), out...  30.2 us
    all_to_all x1, blocking collectives, body(): lax.all_to_all(packed, 'rs', 0, 0, tiled=True, axis_index_groups=[[index...  18.3 us
    pallas_call x1, Pallas kernels, mask(): pl.pallas_call(mask_kernel, out_shape=jax.ShapeDtypeStruct((rows, cols),...  7.41 us
    unnamed x36, local copies, waits for them, and re-layouts  7.11 us
  transfers between devices with their start and end apart: 28, of which 11 were waited for; matrix products, arithmetic and copies ran while one was open for 2% of the time, Pallas kernels for 23%

profile of v1, /device:TPU:16, one launch (start us, length us, event | category | flops | bytes accessed | tf_op | source)
XLA Modules:
  0.0 164.9 jit_solution(8962706769466010136)
XLA Ops:
  0.0 3.3 %collective-permute-start.5 = (bf16[64,4096]{1,0:T(8,128)(2,1)}, bf16[64,4096]{1,0:T(8,128)(2,1)S(1)}, u32[]{:S(2)}, u32[]{:S(2)}) collective-permute-start(bf16[64,4096]{1,0:T(8,128)(2,1)} %bitcast.14), channel_id=1, source_target_pairs={{0,64},{16,80},{32,96},{48,112},{64,128},{80,144},{96,160},{112,17... | collective-permute-start | bytes 1572872 | tf_op jit(solution)/shard_map/ppermute | solution.py:21
  6.5 3.0 %collective-permute-start.6 = (bf16[64,4096]{1,0:T(8,128)(2,1)}, bf16[64,4096]{1,0:T(8,128)(2,1)S(1)}, u32[]{:S(2)}, u32[]{:S(2)}) collective-permute-start(bf16[64,4096]{1,0:T(8,128)(2,1)} %bitcast.17), channel_id=1, source_target_pairs={{0,192},{16,208},{32,224},{48,240},{64,0},{80,16},{96,32},{112,48}... | collective-permute-start | bytes 1572872 | tf_op jit(solution)/shard_map/ppermute | solution.py:21
  9.5 13.3 %collective-permute-done.5.refs_0_ = bf16[64,4096]{1,0:T(8,128)(2,1)S(1)} collective-permute-done((bf16[64,4096]{1,0:T(8,128)(2,1)}, bf16[64,4096]{1,0:T(8,128)(2,1)S(1)}, u32[]{:S(2)}, u32[]{:S(2)}) %collective-permute-start.5) | collective-permute-done | bytes 524320 | tf_op jit(solution)/shard_map/ppermute | solution.py:21
  22.8 7.7 %collective-permute-start.10 = (bf16[32,4096]{1,0:T(8,128)(2,1)S(1)}, bf16[32,4096]{1,0:T(8,128)(2,1)S(1)}, u32[]{:S(2)}, u32[]{:S(2)}) collective-permute-start(bf16[32,4096]{1,0:T(8,128)(2,1)S(1)} %slice.26), channel_id=1, source_target_pairs={{0,64},{16,80},{32,96},{48,112},{64,128},{80,144},{96,160},{112,17... | collective-permute-start | bytes 786440 | tf_op jit(solution)/shard_map/ppermute | solution.py:21
  34.0 2.3 %collective-permute-start.11 = (bf16[32,4096]{1,0:T(8,128)(2,1)S(1)}, bf16[32,4096]{1,0:T(8,128)(2,1)S(1)}, u32[]{:S(2)}, u32[]{:S(2)}) collective-permute-start(bf16[32,4096]{1,0:T(8,128)(2,1)S(1)} %slice.27), channel_id=1, source_target_pairs={{0,192},{16,208},{32,224},{48,240},{64,0},{80,16},{96,32},{112,48}... | collective-permute-start | bytes 786440 | tf_op jit(solution)/shard_map/ppermute | solution.py:21
  36.6 5.8 %collective-permute-done.10 = bf16[32,4096]{1,0:T(8,128)(2,1)S(1)} collective-permute-done((bf16[32,4096]{1,0:T(8,128)(2,1)S(1)}, bf16[32,4096]{1,0:T(8,128)(2,1)S(1)}, u32[]{:S(2)}, u32[]{:S(2)}) %collective-permute-start.10) | collective-permute-done | bytes 262176 | tf_op jit(solution)/shard_map/ppermute | solution.py:21
  42.4 2.8 %collective-permute-start.20 = (bf16[64,4096]{1,0:T(8,128)(2,1)S(1)}, bf16[64,4096]{1,0:T(8,128)(2,1)S(1)}, u32[]{:S(2)}, u32[]{:S(2)}) collective-permute-start(bf16[64,4096]{1,0:T(8,128)(2,1)S(1)} %collective-permute-done.5.refs_0_), channel_id=1, source_target_pairs={{0,48},{16,0},{32,16},{48,32},{64,112},{80,64},{96,80},{112,96},{1... | collective-permute-start | bytes 1572872 | tf_op jit(solution)/shard_map/ppermute | solution.py:21
  45.2 2.8 %collective-permute-done.11 = bf16[32,4096]{1,0:T(8,128)(2,1)S(1)} collective-permute-done((bf16[32,4096]{1,0:T(8,128)(2,1)S(1)}, bf16[32,4096]{1,0:T(8,128)(2,1)S(1)}, u32[]{:S(2)}, u32[]{:S(2)}) %collective-permute-start.11) | collective-permute-done | bytes 262176 | tf_op jit(solution)/shard_map/ppermute | solution.py:21
  48.4 3.0 %collective-permute-start.17 = (bf16[64,4096]{1,0:T(8,128)(2,1)S(1)}, bf16[64,4096]{1,0:T(8,128)(2,1)S(1)}, u32[]{:S(2)}, u32[]{:S(2)}) collective-permute-start(bf16[64,4096]{1,0:T(8,128)(2,1)S(1)} %constant_dynamic-update-slice_fusion.2.refs_0_), channel_id=1, source_target_pairs={{0,48},{16,0},{32,16},{48,32},{64,112},{80,64},{96,80},{112,96},{1... | collective-permute-start | bytes 1572872 | tf_op jit(solution)/shard_map/ppermute | solution.py:21
  52.8 3.8 %collective-permute-start.14 = (bf16[64,4096]{1,0:T(8,128)(2,1)}, bf16[64,4096]{1,0:T(8,128)(2,1)S(1)}, u32[]{:S(2)}, u32[]{:S(2)}) collective-permute-start(bf16[64,4096]{1,0:T(8,128)(2,1)} %constant_dynamic-update-slice_fusion.refs_1_), channel_id=1, source_target_pairs={{0,64},{16,80},{32,96},{48,112},{64,128},{80,144},{96,160},{112,17... | collective-permute-start | bytes 1572872 | tf_op jit(solution)/shard_map/ppermute | solution.py:21
  56.6 6.5 %collective-permute-done.12.refs_1_ = bf16[64,4096]{1,0:T(8,128)(2,1)S(1)} collective-permute-done((bf16[64,4096]{1,0:T(8,128)(2,1)S(1)}, bf16[64,4096]{1,0:T(8,128)(2,1)S(1)}, u32[]{:S(2)}, u32[]{:S(2)}) %collective-permute-start.12) | collective-permute-done | bytes 524320 | tf_op jit(solution)/shard_map/ppermute | solution.py:21
  66.3 3.1 %collective-permute-start.18 = (bf16[32,4096]{1,0:T(8,128)(2,1)}, bf16[32,4096]{1,0:T(8,128)(2,1)}, u32[]{:S(2)}, u32[]{:S(2)}) collective-permute-start(bf16[32,4096]{1,0:T(8,128)(2,1)} %slice.29), channel_id=1, source_target_pairs={{0,48},{16,0},{32,16},{48,32},{64,112},{80,64},{96,80},{112,96},{1... | collective-permute-start | bytes 786440 | tf_op jit(solution)/shard_map/ppermute | solution.py:21
  70.2 3.8 %collective-permute-done.14.refs_0_ = bf16[64,4096]{1,0:T(8,128)(2,1)S(1)} collective-permute-done((bf16[64,4096]{1,0:T(8,128)(2,1)}, bf16[64,4096]{1,0:T(8,128)(2,1)S(1)}, u32[]{:S(2)}, u32[]{:S(2)}) %collective-permute-start.14) | collective-permute-done | bytes 524320 | tf_op jit(solution)/shard_map/ppermute | solution.py:21
  75.8 7.4 %shard_map.46.a_ref = bf16[1024,4096]{1,0:T(8,128)(2,1)S(1)} custom-call(s32[8,32]{1,0:T(8,128)S(1)} %bitcast.19, bf16[1024,4096]{1,0:T(8,128)(2,1)} %bitcast.20), custom_call_target="tpu_custom_call" | custom-call | flops 4194304 | bytes 16777216 | tf_op jit(solution)/shard_map/pallas_call | solution.py:46
  83.2 3.5 %collective-permute-done.15.refs_1_ = bf16[64,4096]{1,0:T(8,128)(2,1)} collective-permute-done((bf16[64,4096]{1,0:T(8,128)(2,1)}, bf16[64,4096]{1,0:T(8,128)(2,1)}, u32[]{:S(2)}, u32[]{:S(2)}) %collective-permute-start.15) | collective-permute-done | bytes 524320 | tf_op jit(solution)/shard_map/ppermute | solution.py:21
  86.7 8.1 %shard_map.50 = (f32[192,1024]{1,0:T(8,128)S(1)}, f32[192,1024]{1,0:T(8,128)}) custom-call(s32[1]{0:T(128)} %bitcast.10.swap_ref, bf16[1024,4096]{1,0:T(8,128)(2,1)S(1)} %shard_map.46.a_ref, bf16[64,4096]{1,0:T(8,128)(2,1)S(1)} %copy-done.16, bf16[64,4096]{1,0:T(8,128)(2,1)} %collective-permute-done.15.refs_1_, ...), custom_call_target="tpu_custom_call" | custom-call | flops 3221225472 | bytes 13107200 | tf_op jit(solution)/shard_map/pallas_call | solution.py:81
  94.8 8.0 %shard_map.47 = (f32[128,1024]{1,0:T(8,128)S(1)}, f32[128,1024]{1,0:T(8,128)}) custom-call(s32[1]{0:T(128)} %bitcast.10.swap_ref, bf16[1024,4096]{1,0:T(8,128)(2,1)S(1)} %shard_map.46.a_ref, bf16[64,4096]{1,0:T(8,128)(2,1)S(1)} %bitcast.18, bf16[64,4096]{1,0:T(8,128)(2,1)} %constant_dynamic-update-slice_fusion.refs_1_, ...), custom_call_target="tpu_custom_call" | custom-call | flops 2147483648 | bytes 11534336 | tf_op jit(solution)/shard_map/pallas_call | solution.py:81
  103.0 7.9 %shard_map.48 = (f32[128,1024]{1,0:T(8,128)S(1)}, f32[128,1024]{1,0:T(8,128)}) custom-call(s32[1]{0:T(128)} %bitcast.10.swap_ref, bf16[1024,4096]{1,0:T(8,128)(2,1)S(1)} %shard_map.46.a_ref, bf16[64,4096]{1,0:T(8,128)(2,1)S(1)} %collective-permute-done.5.refs_0_, bf16[64,4096]{1,0:T(8,128)(2,1)S(1)} %collective-permute-done.6.refs_1_, ...), custom_call_target="tpu_custom_call" | custom-call | flops 2147483648 | bytes 11534336 | tf_op jit(solution)/shard_map/pallas_call | solution.py:81
  111.4 6.2 %shard_map.49 = (f32[64,1024]{1,0:T(8,128)S(1)}, f32[64,1024]{1,0:T(8,128)}) custom-call(s32[1]{0:T(128)} %bitcast.10.swap_ref, bf16[1024,4096]{1,0:T(8,128)(2,1)S(1)} %shard_map.46.a_ref, bf16[64,4096]{1,0:T(8,128)(2,1)S(1)} %constant_dynamic-update-slice_fusion.2.refs_0_, bf16[64,4096]{1,0:T(8,128)(2,1)S(1)} %collective-permute-done.12.refs_1_), custom_call_target="tpu_custom_call" | custom-call | flops 1073741824 | bytes 9961472 | tf_op jit(solution)/shard_map/pallas_call | solution.py:81
  124.2 18.3 %all_to_all.5.got_ref = bf16[8,64,1024]{2,1,0:T(8,128)(2,1)S(1)} all-to-all(bf16[8,64,1024]{2,1,0:T(8,128)(2,1)S(1)} %shard_map.51), channel_id=1, replica_groups={{0,2,4,6,8,10,12,14},{1,3,5,7,9,11,13,15},{16,18,20,22,24,26,28,30},{17..., dimensions={0} | all-to-all | bytes 2097152 | tf_op jit(solution)/shard_map/all_to_all | solution.py:247
  143.8 2.7 %collective-permute-start.23 = (f32[4,64,128]{2,1,0:T(8,128)S(1)}, f32[4,64,128]{2,1,0:T(8,128)S(1)}, u32[]{:S(2)}, u32[]{:S(2)}) collective-permute-start(f32[4,64,128]{2,1,0:T(8,128)S(1)} %get-tuple-element.31), channel_id=1, source_target_pairs={{0,32},{16,48},{32,0},{48,16},{64,96},{80,112},{96,64},{112,80},{1... | collective-permute-start | bytes 393224 | tf_op jit(solution)/shard_map/ppermute | solution.py:21
  152.1 3.8 %collective-permute-start.25 = (f32[64,128]{1,0:T(8,128)S(1)}, f32[64,128]{1,0:T(8,128)S(1)}, u32[]{:S(2)}, u32[]{:S(2)}) collective-permute-start(f32[64,128]{1,0:T(8,128)S(1)} %get-tuple-element.34), channel_id=1, source_target_pairs={{0,64},{16,80},{32,96},{48,112},{64,128},{80,144},{96,160},{112,17... | collective-permute-start | bytes 98312 | tf_op jit(solution)/shard_map/ppermute | solution.py:21
  155.9 2.8 %collective-permute-start.26 = (f32[64,128]{1,0:T(8,128)S(1)}, f32[64,128]{1,0:T(8,128)S(1)}, u32[]{:S(2)}, u32[]{:S(2)}) collective-permute-start(f32[64,128]{1,0:T(8,128)S(1)} %get-tuple-element.35), channel_id=1, source_target_pairs={{0,128},{16,144},{32,160},{48,176},{64,192},{80,208},{96,224},{112... | collective-permute-start | bytes 98312 | tf_op jit(solution)/shard_map/ppermute | solution.py:21
  158.7 3.2 %collective-permute-start.27 = (f32[64,128]{1,0:T(8,128)S(1)}, f32[64,128]{1,0:T(8,128)S(1)}, u32[]{:S(2)}, u32[]{:S(2)}) collective-permute-start(f32[64,128]{1,0:T(8,128)S(1)} %get-tuple-element.36), channel_id=1, source_target_pairs={{0,192},{16,208},{32,224},{48,240},{64,0},{80,16},{96,32},{112,48}... | collective-permute-start | bytes 98312 | tf_op jit(solution)/shard_map/ppermute | solution.py:21
  (87 shorter events, 31.6 us)
Async XLA Ops:
  0.0 22.8 %collective-permute-start.5 = (bf16[64,4096]{1,0:T(8,128)(2,1)}, bf16[64,4096]{1,0:T(8,128)(2,1)S(1)}, u32[]{:S(2)}, u32[]{:S(2)}) collective-permute-start(bf16[64,4096]{1,0:T(8,128)(2,1)} %bitcast.14), channel_id=1, source_target_pairs={{0,64},{16,80},{32,96},{48,112},{64,128},{80,144},{96,160},{112,17... | collective-permute-start | bytes 1572872 | tf_op jit(solution)/shard_map/ppermute | solution.py:21
  3.3 27.2 %collective-permute-start = (bf16[64,4096]{1,0:T(8,128)(2,1)}, bf16[64,4096]{1,0:T(8,128)(2,1)S(1)}, u32[]{:S(2)}, u32[]{:S(2)}) collective-permute-start(bf16[64,4096]{1,0:T(8,128)(2,1)} %bitcast.15), channel_id=1, source_target_pairs={{0,16},{16,32},{32,48},{48,0},{64,80},{80,96},{96,112},{112,64},{1... | collective-permute-start | bytes 1572872 | tf_op jit(solution)/shard_map/ppermute | solution.py:21
  4.8 27.3 %collective-permute-start.2 = (bf16[64,4096]{1,0:T(8,128)(2,1)}, bf16[64,4096]{1,0:T(8,128)(2,1)S(1)}, u32[]{:S(2)}, u32[]{:S(2)}) collective-permute-start(bf16[64,4096]{1,0:T(8,128)(2,1)} %bitcast.16), channel_id=1, source_target_pairs={{0,48},{16,0},{32,16},{48,32},{64,112},{80,64},{96,80},{112,96},{1... | collective-permute-start | bytes 1572872 | tf_op jit(solution)/shard_map/ppermute | solution.py:21
  6.5 27.4 %collective-permute-start.6 = (bf16[64,4096]{1,0:T(8,128)(2,1)}, bf16[64,4096]{1,0:T(8,128)(2,1)S(1)}, u32[]{:S(2)}, u32[]{:S(2)}) collective-permute-start(bf16[64,4096]{1,0:T(8,128)(2,1)} %bitcast.17), channel_id=1, source_target_pairs={{0,192},{16,208},{32,224},{48,240},{64,0},{80,16},{96,32},{112,48}... | collective-permute-start | bytes 1572872 | tf_op jit(solution)/shard_map/ppermute | solution.py:21
  22.8 19.6 %collective-permute-start.10 = (bf16[32,4096]{1,0:T(8,128)(2,1)S(1)}, bf16[32,4096]{1,0:T(8,128)(2,1)S(1)}, u32[]{:S(2)}, u32[]{:S(2)}) collective-permute-start(bf16[32,4096]{1,0:T(8,128)(2,1)S(1)} %slice.26), channel_id=1, source_target_pairs={{0,64},{16,80},{32,96},{48,112},{64,128},{80,144},{96,160},{112,17... | collective-permute-start | bytes 786440 | tf_op jit(solution)/shard_map/ppermute | solution.py:21
  30.5 17.9 %collective-permute-start.1 = (bf16[32,4096]{1,0:T(8,128)(2,1)S(1)}, bf16[32,4096]{1,0:T(8,128)(2,1)S(1)}, u32[]{:S(2)}, u32[]{:S(2)}) collective-permute-start(bf16[32,4096]{1,0:T(8,128)(2,1)S(1)} %slice.24), channel_id=1, source_target_pairs={{0,16},{16,32},{32,48},{48,0},{64,80},{80,96},{96,112},{112,64},{1... | collective-permute-start | bytes 786440 | tf_op jit(solution)/shard_map/ppermute | solution.py:21
  32.1 19.9 %collective-permute-start.3 = (bf16[32,4096]{1,0:T(8,128)(2,1)S(1)}, bf16[32,4096]{1,0:T(8,128)(2,1)S(1)}, u32[]{:S(2)}, u32[]{:S(2)}) collective-permute-start(bf16[32,4096]{1,0:T(8,128)(2,1)S(1)} %slice.25), channel_id=1, source_target_pairs={{0,48},{16,0},{32,16},{48,32},{64,112},{80,64},{96,80},{112,96},{1... | collective-permute-start | bytes 786440 | tf_op jit(solution)/shard_map/ppermute | solution.py:21
  34.0 14.0 %collective-permute-start.11 = (bf16[32,4096]{1,0:T(8,128)(2,1)S(1)}, bf16[32,4096]{1,0:T(8,128)(2,1)S(1)}, u32[]{:S(2)}, u32[]{:S(2)}) collective-permute-start(bf16[32,4096]{1,0:T(8,128)(2,1)S(1)} %slice.27), channel_id=1, source_target_pairs={{0,192},{16,208},{32,224},{48,240},{64,0},{80,16},{96,32},{112,48}... | collective-permute-start | bytes 786440 | tf_op jit(solution)/shard_map/ppermute | solution.py:21
  36.3 29.1 %collective-permute-start.19 = (bf16[64,4096]{1,0:T(8,128)(2,1)S(1)}, bf16[64,4096]{1,0:T(8,128)(2,1)S(1)}, u32[]{:S(2)}, u32[]{:S(2)}) collective-permute-start(bf16[64,4096]{1,0:T(8,128)(2,1)S(1)} %collective-permute-done.5.refs_0_), channel_id=1, source_target_pairs={{0,16},{16,32},{32,48},{48,0},{64,80},{80,96},{96,112},{112,64},{1... | collective-permute-start | bytes 1572872 | tf_op jit(solution)/shard_map/ppermute | solution.py:21
  42.4 26.9 %collective-permute-start.20 = (bf16[64,4096]{1,0:T(8,128)(2,1)S(1)}, bf16[64,4096]{1,0:T(8,128)(2,1)S(1)}, u32[]{:S(2)}, u32[]{:S(2)}) collective-permute-start(bf16[64,4096]{1,0:T(8,128)(2,1)S(1)} %collective-permute-done.5.refs_0_), channel_id=1, source_target_pairs={{0,48},{16,0},{32,16},{48,32},{64,112},{80,64},{96,80},{112,96},{1... | collective-permute-start | bytes 1572872 | tf_op jit(solution)/shard_map/ppermute | solution.py:21
  48.0 15.1 %collective-permute-start.12 = (bf16[64,4096]{1,0:T(8,128)(2,1)S(1)}, bf16[64,4096]{1,0:T(8,128)(2,1)S(1)}, u32[]{:S(2)}, u32[]{:S(2)}) collective-permute-start(bf16[64,4096]{1,0:T(8,128)(2,1)S(1)} %constant_dynamic-update-slice_fusion.2.refs_0_), channel_id=1, source_target_pairs={{0,16},{16,32},{32,48},{48,0},{64,80},{80,96},{96,112},{112,64},{1... | collective-permute-start | bytes 1572872 | tf_op jit(solution)/shard_map/ppermute | solution.py:21
  48.4 16.2 %collective-permute-start.17 = (bf16[64,4096]{1,0:T(8,128)(2,1)S(1)}, bf16[64,4096]{1,0:T(8,128)(2,1)S(1)}, u32[]{:S(2)}, u32[]{:S(2)}) collective-permute-start(bf16[64,4096]{1,0:T(8,128)(2,1)S(1)} %constant_dynamic-update-slice_fusion.2.refs_0_), channel_id=1, source_target_pairs={{0,48},{16,0},{32,16},{48,32},{64,112},{80,64},{96,80},{112,96},{1... | collective-permute-start | bytes 1572872 | tf_op jit(solution)/shard_map/ppermute | solution.py:21
  52.8 21.2 %collective-permute-start.14 = (bf16[64,4096]{1,0:T(8,128)(2,1)}, bf16[64,4096]{1,0:T(8,128)(2,1)S(1)}, u32[]{:S(2)}, u32[]{:S(2)}) collective-permute-start(bf16[64,4096]{1,0:T(8,128)(2,1)} %constant_dynamic-update-slice_fusion.refs_1_), channel_id=1, source_target_pairs={{0,64},{16,80},{32,96},{48,112},{64,128},{80,144},{96,160},{112,17... | collective-permute-start | bytes 1572872 | tf_op jit(solution)/shard_map/ppermute | solution.py:21
  63.1 23.6 %collective-permute-start.15 = (bf16[64,4096]{1,0:T(8,128)(2,1)}, bf16[64,4096]{1,0:T(8,128)(2,1)}, u32[]{:S(2)}, u32[]{:S(2)}) collective-permute-start(bf16[64,4096]{1,0:T(8,128)(2,1)} %constant_dynamic-update-slice_fusion.refs_1_), channel_id=1, source_target_pairs={{0,192},{16,208},{32,224},{48,240},{64,0},{80,16},{96,32},{112,48}... | collective-permute-start | bytes 1572872 | tf_op jit(solution)/shard_map/ppermute | solution.py:21
  64.5 22.1 %collective-permute-start.16 = (bf16[32,4096]{1,0:T(8,128)(2,1)}, bf16[32,4096]{1,0:T(8,128)(2,1)S(1)}, u32[]{:S(2)}, u32[]{:S(2)}) collective-permute-start(bf16[32,4096]{1,0:T(8,128)(2,1)} %slice.28), channel_id=1, source_target_pairs={{0,16},{16,32},{32,48},{48,0},{64,80},{80,96},{96,112},{112,64},{1... | collective-permute-start | bytes 786440 | tf_op jit(solution)/shard_map/ppermute | solution.py:21
  66.3 20.4 %collective-permute-start.18 = (bf16[32,4096]{1,0:T(8,128)(2,1)}, bf16[32,4096]{1,0:T(8,128)(2,1)}, u32[]{:S(2)}, u32[]{:S(2)}) collective-permute-start(bf16[32,4096]{1,0:T(8,128)(2,1)} %slice.29), channel_id=1, source_target_pairs={{0,48},{16,0},{32,16},{48,32},{64,112},{80,64},{96,80},{112,96},{1... | collective-permute-start | bytes 786440 | tf_op jit(solution)/shard_map/ppermute | solution.py:21
  70.2 32.9 %collective-permute-start.7 = (bf16[64,4096]{1,0:T(8,128)(2,1)S(1)}, bf16[64,4096]{1,0:T(8,128)(2,1)}, u32[]{:S(2)}, u32[]{:S(2)}) collective-permute-start(bf16[64,4096]{1,0:T(8,128)(2,1)S(1)} %collective-permute-done.6.refs_1_), channel_id=1, source_target_pairs={{0,16},{16,32},{32,48},{48,0},{64,80},{80,96},{96,112},{112,64},{1... | collective-permute-start | bytes 1572872 | tf_op jit(solution)/shard_map/ppermute | solution.py:21
  74.8 28.3 %collective-permute-start.8 = (bf16[64,4096]{1,0:T(8,128)(2,1)S(1)}, bf16[64,4096]{1,0:T(8,128)(2,1)}, u32[]{:S(2)}, u32[]{:S(2)}) collective-permute-start(bf16[64,4096]{1,0:T(8,128)(2,1)S(1)} %collective-permute-done.6.refs_1_), channel_id=1, source_target_pairs={{0,48},{16,0},{32,16},{48,32},{64,112},{80,64},{96,80},{112,96},{1... | collective-permute-start | bytes 1572872 | tf_op jit(solution)/shard_map/ppermute | solution.py:21
  94.8 24.6 %collective-permute-start.21 = (f32[192,1024]{1,0:T(8,128)}, f32[192,1024]{1,0:T(8,128)}, u32[]{:S(2)}, u32[]{:S(2)}) collective-permute-start(f32[192,1024]{1,0:T(8,128)} %get-tuple-element.28), channel_id=1, source_target_pairs={{0,1},{1,0},{2,3},{3,2},{4,5},{5,4},{6,7},{7,6},{8,9},{9,8},{10,11... | collective-permute-start | bytes 2359304 | tf_op jit(solution)/shard_map/ppermute | solution.py:25
  102.8 15.2 %collective-permute-start.4 = (f32[128,1024]{1,0:T(8,128)}, f32[128,1024]{1,0:T(8,128)}, u32[]{:S(2)}, u32[]{:S(2)}) collective-permute-start(f32[128,1024]{1,0:T(8,128)} %get-tuple-element.22), channel_id=1, source_target_pairs={{0,1},{1,0},{2,3},{3,2},{4,5},{5,4},{6,7},{7,6},{8,9},{9,8},{10,11... | collective-permute-start | bytes 1572872 | tf_op jit(solution)/shard_map/ppermute | solution.py:25
  111.0 7.0 %collective-permute-start.9 = (f32[128,1024]{1,0:T(8,128)}, f32[128,1024]{1,0:T(8,128)}, u32[]{:S(2)}, u32[]{:S(2)}) collective-permute-start(f32[128,1024]{1,0:T(8,128)} %get-tuple-element.24), channel_id=1, source_target_pairs={{0,1},{1,0},{2,3},{3,2},{4,5},{5,4},{6,7},{7,6},{8,9},{9,8},{10,11... | collective-permute-start | bytes 1572872 | tf_op jit(solution)/shard_map/ppermute | solution.py:25
  143.8 7.7 %collective-permute-start.23 = (f32[4,64,128]{2,1,0:T(8,128)S(1)}, f32[4,64,128]{2,1,0:T(8,128)S(1)}, u32[]{:S(2)}, u32[]{:S(2)}) collective-permute-start(f32[4,64,128]{2,1,0:T(8,128)S(1)} %get-tuple-element.31), channel_id=1, source_target_pairs={{0,32},{16,48},{32,0},{48,16},{64,96},{80,112},{96,64},{112,80},{1... | collective-permute-start | bytes 393224 | tf_op jit(solution)/shard_map/ppermute | solution.py:21
  152.1 9.8 %collective-permute-start.25 = (f32[64,128]{1,0:T(8,128)S(1)}, f32[64,128]{1,0:T(8,128)S(1)}, u32[]{:S(2)}, u32[]{:S(2)}) collective-permute-start(f32[64,128]{1,0:T(8,128)S(1)} %get-tuple-element.34), channel_id=1, source_target_pairs={{0,64},{16,80},{32,96},{48,112},{64,128},{80,144},{96,160},{112,17... | collective-permute-start | bytes 98312 | tf_op jit(solution)/shard_map/ppermute | solution.py:21
  155.9 8.3 %collective-permute-start.26 = (f32[64,128]{1,0:T(8,128)S(1)}, f32[64,128]{1,0:T(8,128)S(1)}, u32[]{:S(2)}, u32[]{:S(2)}) collective-permute-start(f32[64,128]{1,0:T(8,128)S(1)} %get-tuple-element.35), channel_id=1, source_target_pairs={{0,128},{16,144},{32,160},{48,176},{64,192},{80,208},{96,224},{112... | collective-permute-start | bytes 98312 | tf_op jit(solution)/shard_map/ppermute | solution.py:21
  (21 other events, 156.1 us)

commit v2 on v1

v2 whole, which is shorter than its diff:
```python
import functools

import jax
import jax.numpy as jnp
from jax import lax
from jax.experimental import pallas as pl
from jax.experimental.pallas import tpu as pltpu
from jax.sharding import PartitionSpec as P

TILE = 128
F32 = jnp.float32
BF16 = jnp.bfloat16
VMEM_LIMIT = 14 * 1024 * 1024
WIDTH = 256
TOKEN = jax.ShapeDtypeStruct((8, 128), F32)


def pq_shift(value, dz, dx):
    perm = []
    for index in range(16):
        z, x = divmod(index, 4)
        perm.append((index, (z + dz) % 4 * 4 + (x + dx) % 4))
    return lax.ppermute(value, "pq", perm)


def send(value, dz, dx):
    perm = []
    for index in range(256):
        pq_at, rs_at = divmod(index, 16)
        z, x = divmod(pq_at, 4)
        sign = 1 if rs_at % 2 == 0 else -1
        perm.append((index, ((z + sign * dz) % 4 * 4 + (x + sign * dx) % 4) * 16 + rs_at))
    return lax.ppermute(value, ("pq", "rs"), perm)


def after(value, *others):
    return lax.optimization_barrier((value,) + others)[0]


SHIFTS = [(0, 0), (0, 1), (1, 0), (1, 1), (2, 0), (2, 1), (3, 0), (3, 1)]


def rs_send(value, dy, dl):
    perm = []
    for index in range(16):
        y, rest = divmod(index, 4)
        sign = 1 if index % 2 == 0 else -1
        perm.append((index, (y + sign * dy) % 4 * 4 + rest ^ (dl * 2)))
    return lax.ppermute(value, "rs", perm)


def core_swap(value):
    return lax.ppermute(value, "rs", [(index, index ^ 1) for index in range(16)])


def params():
    return pltpu.CompilerParams(vmem_limit_bytes=VMEM_LIMIT)


def cost(flops, bytes_accessed):
    return pl.CostEstimate(flops=flops, bytes_accessed=bytes_accessed, transcendentals=0)


def mask_kernel(screen_ref, a_ref, out_ref, token_ref):
    at = pl.program_id(0)
    token_ref[...] = jnp.zeros(token_ref.shape, F32)
    for col in range(a_ref.shape[1] // TILE):
        cols = slice(col * TILE, (col + 1) * TILE)
        for row in range(WIDTH // TILE):
            rows = slice(row * TILE, (row + 1) * TILE)
            flag = screen_ref[at * (WIDTH // TILE) + row, col].astype(F32)
            out_ref[0, cols, rows] = (a_ref[rows, cols].astype(F32) * flag).T.astype(BF16)


def mask(integrals, screen):
    rows, cols = integrals.shape
    return pl.pallas_call(
        mask_kernel,
        out_shape=[jax.ShapeDtypeStruct((rows // WIDTH, cols, WIDTH), BF16), TOKEN],
        grid_spec=pltpu.PrefetchScalarGridSpec(
            num_scalar_prefetch=1,
            grid=(rows // WIDTH,),
            in_specs=[pl.BlockSpec((WIDTH, cols), lambda at, _: (at, 0))],
            out_specs=[
                pl.BlockSpec((1, cols, WIDTH), lambda at, _: (at, 0, 0)),
                pl.BlockSpec(TOKEN.shape, lambda at, _: (0, 0)),
            ],
        ),
        compiler_params=params(),
        cost_estimate=cost(rows * cols, 4 * rows * cols),
    )(screen, integrals)


def half_kernel(swap_ref, a_ref, *refs):
    pieces, (keep_ref, send_ref) = refs[:4], refs[-2:]
    n = keep_ref.shape[0]
    swap = swap_ref[0] != 0
    coeff = jnp.concatenate([ref[...] for ref in pieces], axis=0)
    for at in range(a_ref.shape[0]):
        cols = slice(at * WIDTH, (at + 1) * WIDTH)
        product = jnp.dot(coeff, a_ref[at], preferred_element_type=F32)
        even, odd = product[:n], product[n:]
        keep_ref[:, cols] = jnp.where(swap, odd, even)
        send_ref[:, cols] = jnp.where(swap, even, odd)


def half_transform(swap, masked, even, odd, waits=()):
    count, cols, width = masked.shape
    rows = count * width
    pieces = list(even) + list(odd)
    n = len(even) * 64
    out = jax.ShapeDtypeStruct((n, rows), F32)
    return pl.pallas_call(
        half_kernel,
        out_shape=[out, out],
        in_specs=[pl.BlockSpec(memory_space=pltpu.SMEM)]
        + [pl.BlockSpec(memory_space=pltpu.VMEM)] * (1 + len(pieces))
        + [pl.BlockSpec(memory_space=pl.ANY)] * len(waits),
        out_specs=[pl.BlockSpec(memory_space=pltpu.VMEM)] * 2,
        compiler_params=params(),
        cost_estimate=cost(4 * n * rows * cols, 2 * rows * cols + 4 * n * cols + 8 * n * rows),
    )(swap, masked, *pieces, *waits)


def pack_kernel(keep_at_ref, got_at_ref, *refs):
    inputs, outs, total_ref = refs[:8], refs[8:16], refs[16]
    for at in range(4):
        for row in range(2):
            rows = slice(row * 64, (row + 1) * 64)
            total_ref[keep_at_ref[at * 2 + row]] = inputs[at * 2][rows, :]
    for at in range(4):
        for row in range(2):
            rows = slice(row * 64, (row + 1) * 64)
            total_ref[got_at_ref[at * 2 + row]] += inputs[at * 2 + 1][rows, :]
    for at in range(8):
        outs[at][...] = total_ref[at].astype(outs[at].dtype)


def pack(keep_at, got_at, pairs):
    flat = [value for pair in pairs for value in pair]
    rows = flat[0].shape[1]
    return pl.pallas_call(
        pack_kernel,
        out_shape=[jax.ShapeDtypeStruct((64, rows), F32 if at == 0 else BF16) for at in range(8)],
        in_specs=[pl.BlockSpec(memory_space=pltpu.SMEM)] * 2
        + [pl.BlockSpec(memory_space=pltpu.VMEM)] * 8,
        out_specs=[pl.BlockSpec(memory_space=pltpu.VMEM)] * 8,
        scratch_shapes=[pltpu.VMEM((8, 64, rows), F32)],
        compiler_params=params(),
        cost_estimate=cost(8 * 64 * rows, 10 * 8 * 64 * rows),
    )(keep_at, got_at, *flat)


def second_kernel(x_ref, *refs):
    gots, coeff_ref, outs, turned_ref = refs[:8], refs[8], refs[9:13], refs[13]
    half = gots[0][...]
    for ref in gots[1:]:
        half = half + ref[...].astype(F32)
    high = half.astype(BF16)
    low = (half - high.astype(F32)).astype(BF16)
    parts = []
    for slab in range(2):
        at = slice(slab * 512, (slab + 1) * 512)
        coeff = coeff_ref[slab]
        both = jnp.concatenate([high[:, at], low[:, at]], axis=0)
        product = jnp.dot(both, coeff, preferred_element_type=F32)
        parts.append(product[:64] + product[64:])
    turned_ref[...] = jnp.concatenate(parts, axis=0).T
    for dx in range(4):
        x = lax.rem(x_ref[0] + dx, 4)
        for z in range(4):
            first = pl.multiple_of((z * 4 + x) * 64, 64)
            outs[dx][z] = turned_ref[pl.ds(first, 64), :].astype(outs[dx].dtype)


def second_transform(x, gots, pq_coeff):
    return pl.pallas_call(
        second_kernel,
        out_shape=[jax.ShapeDtypeStruct((4, 64, 128), F32) for at in range(4)],
        in_specs=[pl.BlockSpec(memory_space=pltpu.SMEM)]
        + [pl.BlockSpec(memory_space=pltpu.VMEM)] * 9,
        out_specs=[pl.BlockSpec(memory_space=pltpu.VMEM)] * 4,
        scratch_shapes=[pltpu.VMEM((1024, 128), F32)],
        compiler_params=params(),
        cost_estimate=cost(8 * 64 * 512 * 1024, 4 * 1024 * 1024),
    )(x, *gots, pq_coeff)


def turn_kernel(z_ref, a_ref, b_ref, c_ref, d_ref, *outs):
    for dz in range(4):
        z = lax.rem(z_ref[0] + dz, 4)
        near = b_ref[z].astype(F32) + c_ref[z].astype(F32)
        outs[dz][...] = a_ref[z] + (near + d_ref[z].astype(F32))


def turn(z, parts):
    out = jax.ShapeDtypeStruct((64, 128), F32)
    return pl.pallas_call(
        turn_kernel,
        out_shape=[out] * 4,
        in_specs=[pl.BlockSpec(memory_space=pltpu.SMEM)]
        + [pl.BlockSpec(memory_space=pltpu.VMEM)] * 4,
        out_specs=[pl.BlockSpec(memory_space=pltpu.VMEM)] * 4,
        compiler_params=params(),
        cost_estimate=cost(4 * 64 * 128 * 4, 4 * 64 * 128 * 4 * 5),
    )(z, *parts)


def last_kernel(a_ref, b_ref, c_ref, d_ref, out_ref):
    total = (a_ref[...] + b_ref[...]) + (c_ref[...] + d_ref[...])
    out_ref[0] = total[:, :64]
    out_ref[1] = total[:, 64:]


def last(parts):
    return pl.pallas_call(
        last_kernel,
        out_shape=jax.ShapeDtypeStruct((2, 64, 64), F32),
        in_specs=[pl.BlockSpec(memory_space=pltpu.VMEM)] * 4,
        out_specs=pl.BlockSpec(memory_space=pltpu.VMEM),
        compiler_params=params(),
    )(*parts)


def body(integrals, screen, rs_coeff, pq_coeff):
    slabs, pq_rows, rs_cols = integrals.shape
    pq_at, rs_at = lax.axis_index("pq"), lax.axis_index("rs")
    z, x = pq_at // 4, pq_at % 4
    core = rs_at % 2
    sign = 1 - 2 * core
    swap = (x + core) % 2
    swap_at = swap.astype(jnp.int32).reshape(1)

    own = rs_coeff.T

    block = {(0, 0): own}
    block[0, -1] = send(own, 0, 1)
    block[-1, 0] = send(own, 1, 0)
    block[0, 1] = send(own, 0, -1)
    masked, token = mask(
        integrals.reshape(slabs * pq_rows, rs_cols),
        screen.reshape(slabs * (pq_rows // TILE), rs_cols // TILE),
    )
    x_less, token = lax.optimization_barrier((block[0, -1], token))
    block[0, 2] = send(x_less, 0, 1)
    block[2, 0] = send(block[-1, 0], 1, 0)
    block[-1, -1] = send(after(block[-1, 0], block[0, -1]), 0, 1)
    block[-1, 1] = send(after(block[-1, 0], block[0, 1]), 0, -1)
    block[-1, 2] = send(block[-1, -1], 0, 1)
    block[1, 0] = send(after(own, block[0, 2]), -1, 0)
    first = half_transform(
        swap_at, masked, [own, block[0, 2]], [block[0, -1], block[0, 1]], [token]
    )
    block[2, -1] = send(after(block[2, 0], block[0, 2]), 0, 1)
    block[2, 1] = send(after(block[2, 0], block[-1, -1]), 0, -1)
    block[2, 2] = send(after(block[2, -1], block[-1, 2], block[-1, 1], *first), 0, 1)
    block[1, 2] = send(after(block[0, 2], block[1, 0]), -1, 0)
    block[1, -1] = send(after(block[1, 0], block[2, -1]), 0, 1)
    block[1, 1] = send(after(block[1, 0], block[2, 1]), 0, -1)
    second = half_transform(
        swap_at, masked, [block[-1, 0], block[-1, 2]], [block[-1, -1], block[-1, 1]], first
    )
    third = half_transform(
        swap_at, masked, [block[2, 0], block[2, 2]], [block[2, -1], block[2, 1]], second
    )
    fourth = half_transform(
        swap_at, masked, [block[1, 0], block[1, 2]], [block[1, -1], block[1, 1]], third
    )
    halves = [first, second, third, fourth]
    places = [((dz, even), (dz, odd)) for dz in (0, -1, 2, 1) for even, odd in ((0, -1), (2, 1))]

    def slot(place, sign):
        to = (z + sign * place[0] + 4) % 4, (x + sign * place[1] + 4) % 4
        shift = (one * (to[0] - y) + 8) % 4 * 2 + (to[1] // 2 - low + 2) % 2
        return sum(
            jnp.where(shift == dy * 2 + dl, at, 0) for at, (dy, dl) in enumerate(SHIFTS)
        )

    one = sign
    y, low = rs_at // 4, rs_at % 4 // 2
    keep_at = jnp.stack([jnp.where(swap == 0, slot(e, one), slot(o, one)) for e, o in places])
    got_at = jnp.stack([jnp.where(swap == 0, slot(e, -one), slot(o, -one)) for e, o in places])
    pairs = [(keep, core_swap(other)) for keep, other in halves]
    gots = list(pack(keep_at.astype(jnp.int32), got_at.astype(jnp.int32), pairs))
    for at in range(1, 8):
        gots[at] = rs_send(gots[at], *SHIFTS[at])
    parts = second_transform(x.astype(jnp.int32).reshape(1), gots, pq_coeff)
    parts = [parts[0]] + [pq_shift(parts[dx], 0, dx) for dx in (1, 2, 3)]
    parts = turn(z.astype(jnp.int32).reshape(1), parts)
    parts = [parts[0]] + [pq_shift(parts[dz], dz, 0) for dz in (1, 2, 3)]
    return last(parts)


def solution(mesh):
    return jax.shard_map(
        body,
        mesh=mesh,
        in_specs=(P(None, "pq", "rs"), P(None, "pq", "rs"), P("rs", "pq"), P(None, "pq", None)),
        out_specs=P(None, "pq", "rs"),
        check_vma=False,
    )
```

time: 167 us -> 134 us (0.80); the launches traced: 165 us -> 134 us
  blocking collectives: 18.3 us -> 0 us
  Pallas kernels: 40.7 us -> 22.7 us
  local copies, waits for them, and re-layouts: 9.56 us -> 18.1 us
  starting transfers between devices: 52.8 us -> 50 us
  waiting for transfers between devices: 43.4 us -> 40.8 us
  between operations: 0.24 us -> 2.14 us
    ppermute x24 -> x6, starting transfers between devices: 52 us -> 12.9 us  [pq_shift(): return lax.ppermute(value, 'pq', perm)]
    ppermute x0 -> x22, starting transfers between devices: none -> 36.6 us  [the longest x15 26.6 us: send(): return lax.ppermute(value, ('pq', 'rs'), perm)]
    ppermute x24 -> x6, waiting for transfers between devices: 42 us -> 10.5 us  [pq_shift(): return lax.ppermute(value, 'pq', perm)]
    ppermute x0 -> x22, waiting for transfers between devices: none -> 30 us  [the longest x15 23.7 us: send(): return lax.ppermute(value, ('pq', 'rs'), perm)]
    all_to_all x1 -> x0, blocking collectives: 18.3 us -> none  [body(): lax.all_to_all(packed, 'rs', 0, 0, tiled=True, axis_index_groups=[[index...]
    pallas_call x7, Pallas kernels: 40 us -> 22 us  [the longest x4 16.3 us: half_transform(): pl.pallas_call(half_kernel, out_shape=[out, out], in_specs=[pl.BlockSpec(...]
    unnamed x36 -> x28, local copies, waits for them, and re-layouts: 7.11 us -> 17.9 us
  transfers between devices with their start and end apart: 28 -> 32, of which waited for: 11 -> 13; matrix products, arithmetic and copies ran while one was open for 2% -> 0% of each run, Pallas kernels for 23% -> 15%
where the time goes in v2:
time: 134 us
  starting transfers between devices  50 us (37%)
  waiting for transfers between devices  40.8 us (30%)
  Pallas kernels  22.7 us (17%)
  local copies, waits for them, and re-layouts  18.1 us (14%)
  between operations  2.14 us (2%)
    ppermute x15, starting transfers between devices, send(): return lax.ppermute(value, ('pq', 'rs'), perm)  26.6 us
    ppermute x15, waiting for transfers between devices, send(): return lax.ppermute(value, ('pq', 'rs'), perm)  23.7 us
    unnamed x28, local copies, waits for them, and re-layouts  17.9 us
    pallas_call x4, Pallas kernels, half_transform(): pl.pallas_call(half_kernel, out_shape=[out, out], in_specs=[pl.BlockSpec(...  16.3 us
    ppermute x6, starting transfers between devices, pq_shift(): return lax.ppermute(value, 'pq', perm)  12.9 us
    ppermute x6, waiting for transfers between devices, pq_shift(): return lax.ppermute(value, 'pq', perm)  10.5 us
    ppermute x7, starting transfers between devices, rs_send(): return lax.ppermute(value, 'rs', perm)  10 us
    ppermute x7, waiting for transfers between devices, rs_send(): return lax.ppermute(value, 'rs', perm)  6.31 us
  transfers between devices with their start and end apart: 32, of which 13 were waited for; matrix products, arithmetic and copies ran while one was open for 0% of the time, Pallas kernels for 15%

profile of v2, /device:TPU:16, one launch (start us, length us, event | category | flops | bytes accessed | tf_op | source)
XLA Modules:
  0.0 133.7 jit_solution(2989562511890262987)
XLA Ops:
  1.5 3.3 %collective-permute-start.4 = (bf16[64,4096]{1,0:T(8,128)(2,1)}, bf16[64,4096]{1,0:T(8,128)(2,1)S(1)}, u32[]{:S(2)}, u32[]{:S(2)}) collective-permute-start(bf16[64,4096]{1,0:T(8,128)(2,1)} %bitcast.24), channel_id=1, source_target_pairs={{0,64},{1,193},{2,66},{3,195},{4,68},{5,197},{6,70},{7,199},{8,72}... | collective-permute-start | bytes 1572872 | tf_op jit(solution)/shard_map/ppermute | solution.py:33
  6.5 3.4 %copy-done.2 = bf16[2,512,4096]{2,1,0:T(8,128)(2,1)S(1)} copy-done((bf16[2,512,4096]{2,1,0:T(8,128)(2,1)S(1)}, bf16[2,512,4096]{2,1,0:T(8,128)(2,1)}, u32[]{:S(2)}) %copy-start.2) | copy-done | bytes 8388632
  10.6 3.3 %shard_map.46 = (bf16[4,4096,256]{2,1,0:T(8,128)(2,1)S(1)}, f32[8,128]{1,0:T(8,128)S(1)}) custom-call(s32[8,32]{1,0:T(8,128)S(1)} %bitcast.28, bf16[1024,4096]{1,0:T(8,128)(2,1)S(1)} %bitcast.22), custom_call_target="tpu_custom_call" | custom-call | flops 4194304 | bytes 16777216 | tf_op jit(solution)/shard_map/pallas_call | solution.py:77
  13.9 3.3 %copy-done = bf16[4,4096,256]{2,1,0:T(8,128)(2,1)} copy-done((bf16[4,4096,256]{2,1,0:T(8,128)(2,1)}, bf16[4,4096,256]{2,1,0:T(8,128)(2,1)S(1)}, u32[]{:S(2)}) %copy-start) | copy-done | bytes 8388632
  18.3 4.5 %collective-permute-start.9 = (bf16[64,4096]{1,0:T(8,128)(2,1)S(1)}, bf16[64,4096]{1,0:T(8,128)(2,1)S(1)}, u32[]{:S(2)}, u32[]{:S(2)}) collective-permute-start(bf16[64,4096]{1,0:T(8,128)(2,1)S(1)} %collective-permute-done.4.refs_0_), channel_id=1, source_target_pairs={{0,64},{1,193},{2,66},{3,195},{4,68},{5,197},{6,70},{7,199},{8,72}... | collective-permute-start | bytes 1572872 | tf_op jit(solution)/shard_map/ppermute | solution.py:33
  27.7 8.8 %collective-permute-done.9.refs_0_ = bf16[64,4096]{1,0:T(8,128)(2,1)S(1)} collective-permute-done((bf16[64,4096]{1,0:T(8,128)(2,1)S(1)}, bf16[64,4096]{1,0:T(8,128)(2,1)S(1)}, u32[]{:S(2)}, u32[]{:S(2)}) %collective-permute-start.9) | collective-permute-done | bytes 524320 | tf_op jit(solution)/shard_map/ppermute | solution.py:33
  39.2 2.1 %collective-permute-start.12 = (bf16[64,4096]{1,0:T(8,128)(2,1)S(1)}, bf16[64,4096]{1,0:T(8,128)(2,1)}, u32[]{:S(2)}, u32[]{:S(2)}) collective-permute-start(bf16[64,4096]{1,0:T(8,128)(2,1)S(1)} %collective-permute-done.9.refs_0_), channel_id=1, source_target_pairs={{0,48},{1,17},{2,50},{3,19},{4,52},{5,21},{6,54},{7,23},{8,56},{9,... | collective-permute-start | bytes 1572872 | tf_op jit(solution)/shard_map/ppermute | solution.py:33
  41.3 3.9 %collective-permute-start.14 = (bf16[64,4096]{1,0:T(8,128)(2,1)S(1)}, bf16[64,4096]{1,0:T(8,128)(2,1)}, u32[]{:S(2)}, u32[]{:S(2)}) collective-permute-start(bf16[64,4096]{1,0:T(8,128)(2,1)S(1)} %bitcast.26), channel_id=1, source_target_pairs={{0,192},{1,65},{2,194},{3,67},{4,196},{5,69},{6,198},{7,71},{8,200... | collective-permute-start | bytes 1572872 | tf_op jit(solution)/shard_map/ppermute | solution.py:33
  45.2 3.4 %copy-done.1 = bf16[4,4096,256]{2,1,0:T(8,128)(2,1)S(1)} copy-done((bf16[4,4096,256]{2,1,0:T(8,128)(2,1)S(1)}, bf16[4,4096,256]{2,1,0:T(8,128)(2,1)}, u32[]{:S(2)}) %copy-start.1) | copy-done | bytes 8388632
  50.6 3.4 %shard_map.47 = (f32[128,1024]{1,0:T(8,128)S(1)}, f32[128,1024]{1,0:T(8,128)S(1)}) custom-call(s32[1]{0:T(128)} %bitcast.18.swap_ref, bf16[4,4096,256]{2,1,0:T(8,128)(2,1)S(1)} %copy-done.1, bf16[64,4096]{1,0:T(8,128)(2,1)S(1)} %bitcast.27, bf16[64,4096]{1,0:T(8,128)(2,1)} %collective-permute-done.1.refs_1_, bf16[64,4096]{1,0:T(8,128)(2,1)S(1)} %copy-done.10, ...), custom_call_target="tpu_custom_call" | custom-call | flops 2147483648 | bytes 11534336 | tf_op jit(solution)/shard_map/pallas_call | solution.py:113
  54.0 4.3 %collective-permute-done.6.refs_1_ = bf16[64,4096]{1,0:T(8,128)(2,1)} collective-permute-done((bf16[64,4096]{1,0:T(8,128)(2,1)S(1)}, bf16[64,4096]{1,0:T(8,128)(2,1)}, u32[]{:S(2)}, u32[]{:S(2)}) %collective-permute-start.6) | collective-permute-done | bytes 524320 | tf_op jit(solution)/shard_map/ppermute | solution.py:33
  58.6 2.8 %collective-permute-done.14.refs_0_ = bf16[64,4096]{1,0:T(8,128)(2,1)} collective-permute-done((bf16[64,4096]{1,0:T(8,128)(2,1)S(1)}, bf16[64,4096]{1,0:T(8,128)(2,1)}, u32[]{:S(2)}, u32[]{:S(2)}) %collective-permute-start.14) | collective-permute-done | bytes 524320 | tf_op jit(solution)/shard_map/ppermute | solution.py:33
  61.5 1.8 %collective-permute-start.16 = (bf16[64,4096]{1,0:T(8,128)(2,1)}, bf16[64,4096]{1,0:T(8,128)(2,1)S(1)}, u32[]{:S(2)}, u32[]{:S(2)}) collective-permute-start(bf16[64,4096]{1,0:T(8,128)(2,1)} %collective-permute-done.14.refs_0_), channel_id=1, source_target_pairs={{0,16},{1,49},{2,18},{3,51},{4,20},{5,53},{6,22},{7,55},{8,24},{9,... | collective-permute-start | bytes 1572872 | tf_op jit(solution)/shard_map/ppermute | solution.py:33
  64.5 4.4 %shard_map.48 = (f32[128,1024]{1,0:T(8,128)S(1)}, f32[128,1024]{1,0:T(8,128)}) custom-call(s32[1]{0:T(128)} %bitcast.18.swap_ref, bf16[4,4096,256]{2,1,0:T(8,128)(2,1)S(1)} %copy-done.1, bf16[64,4096]{1,0:T(8,128)(2,1)S(1)} %collective-permute-done.4.refs_0_, bf16[64,4096]{1,0:T(8,128)(2,1)} %collective-permute-done.6.refs_1_, ...), custom_call_target="tpu_custom_call" | custom-call | flops 2147483648 | bytes 11534336 | tf_op jit(solution)/shard_map/pallas_call | solution.py:113
  68.9 5.6 %collective-permute-done.11.refs_1_ = bf16[64,4096]{1,0:T(8,128)(2,1)S(1)} collective-permute-done((bf16[64,4096]{1,0:T(8,128)(2,1)}, bf16[64,4096]{1,0:T(8,128)(2,1)S(1)}, u32[]{:S(2)}, u32[]{:S(2)}) %collective-permute-start.11) | collective-permute-done | bytes 524320 | tf_op jit(solution)/shard_map/ppermute | solution.py:33
  74.5 4.3 %shard_map.49 = (f32[128,1024]{1,0:T(8,128)S(1)}, f32[128,1024]{1,0:T(8,128)}) custom-call(s32[1]{0:T(128)} %bitcast.18.swap_ref, bf16[4,4096,256]{2,1,0:T(8,128)(2,1)S(1)} %copy-done.1, bf16[64,4096]{1,0:T(8,128)(2,1)S(1)} %copy-done.8, bf16[64,4096]{1,0:T(8,128)(2,1)S(1)} %collective-permute-done.11.refs_1_, ...), custom_call_target="tpu_custom_call" | custom-call | flops 2147483648 | bytes 11534336 | tf_op jit(solution)/shard_map/pallas_call | solution.py:113
  80.2 4.2 %shard_map.50 = (f32[128,1024]{1,0:T(8,128)S(1)}, f32[128,1024]{1,0:T(8,128)}) custom-call(s32[1]{0:T(128)} %bitcast.18.swap_ref, bf16[4,4096,256]{2,1,0:T(8,128)(2,1)S(1)} %copy-done.1, bf16[64,4096]{1,0:T(8,128)(2,1)} %collective-permute-done.14.refs_0_, bf16[64,4096]{1,0:T(8,128)(2,1)S(1)} %collective-permute-done.15.refs_1_, ...), custom_call_target="tpu_custom_call" | custom-call | flops 2147483648 | bytes 11534336 | tf_op jit(solution)/shard_map/pallas_call | solution.py:113
  94.0 2.0 %collective-permute-start.22 = (bf16[64,1024]{1,0:T(8,128)(2,1)S(1)}, bf16[64,1024]{1,0:T(8,128)(2,1)S(1)}, u32[]{:S(2)}, u32[]{:S(2)}) collective-permute-start(bf16[64,1024]{1,0:T(8,128)(2,1)S(1)} %get-tuple-element.67), channel_id=1, source_target_pairs={{0,8},{1,9},{2,10},{3,11},{4,12},{5,13},{6,14},{7,15},{8,0},{9,1},... | collective-permute-start | bytes 393224 | tf_op jit(solution)/shard_map/ppermute | solution.py:49
  101.0 4.7 %collective-permute-done.22.refs_4_ = bf16[64,1024]{1,0:T(8,128)(2,1)S(1)} collective-permute-done((bf16[64,1024]{1,0:T(8,128)(2,1)S(1)}, bf16[64,1024]{1,0:T(8,128)(2,1)S(1)}, u32[]{:S(2)}, u32[]{:S(2)}) %collective-permute-start.22) | collective-permute-done | bytes 131104 | tf_op jit(solution)/shard_map/ppermute | solution.py:49
  109.7 2.7 %collective-permute-start.27 = (f32[4,64,128]{2,1,0:T(8,128)S(1)}, f32[4,64,128]{2,1,0:T(8,128)S(1)}, u32[]{:S(2)}, u32[]{:S(2)}) collective-permute-start(f32[4,64,128]{2,1,0:T(8,128)S(1)} %get-tuple-element.73), channel_id=1, source_target_pairs={{0,32},{16,48},{32,0},{48,16},{64,96},{80,112},{96,64},{112,80},{1... | collective-permute-start | bytes 393224 | tf_op jit(solution)/shard_map/ppermute | solution.py:23
  112.9 5.7 %collective-permute-done.26.b_ref = f32[4,64,128]{2,1,0:T(8,128)S(1)} collective-permute-done((f32[4,64,128]{2,1,0:T(8,128)S(1)}, f32[4,64,128]{2,1,0:T(8,128)S(1)}, u32[]{:S(2)}, u32[]{:S(2)}) %collective-permute-start.26) | collective-permute-done | bytes 131104 | tf_op jit(solution)/shard_map/ppermute | solution.py:23
  119.3 5.9 %collective-permute-start.29 = (f32[64,128]{1,0:T(8,128)S(1)}, f32[64,128]{1,0:T(8,128)S(1)}, u32[]{:S(2)}, u32[]{:S(2)}) collective-permute-start(f32[64,128]{1,0:T(8,128)S(1)} %get-tuple-element.76), channel_id=1, source_target_pairs={{0,64},{16,80},{32,96},{48,112},{64,128},{80,144},{96,160},{112,17... | collective-permute-start | bytes 98312 | tf_op jit(solution)/shard_map/ppermute | solution.py:23
  125.2 3.7 %collective-permute-start.31 = (f32[64,128]{1,0:T(8,128)S(1)}, f32[64,128]{1,0:T(8,128)S(1)}, u32[]{:S(2)}, u32[]{:S(2)}) collective-permute-start(f32[64,128]{1,0:T(8,128)S(1)} %get-tuple-element.78), channel_id=1, source_target_pairs={{0,192},{16,208},{32,224},{48,240},{64,0},{80,16},{96,32},{112,48}... | collective-permute-start | bytes 98312 | tf_op jit(solution)/shard_map/ppermute | solution.py:23
  128.9 4.1 %collective-permute-done.30.c_ref = f32[64,128]{1,0:T(8,128)S(1)} collective-permute-done((f32[64,128]{1,0:T(8,128)S(1)}, f32[64,128]{1,0:T(8,128)S(1)}, u32[]{:S(2)}, u32[]{:S(2)}) %collective-permute-start.30) | collective-permute-done | bytes 32800 | tf_op jit(solution)/shard_map/ppermute | solution.py:23
  (79 shorter events, 36.1 us)
Async XLA Ops:
  0.0 17.2 %collective-permute-start = (bf16[64,4096]{1,0:T(8,128)(2,1)}, bf16[64,4096]{1,0:T(8,128)(2,1)S(1)}, u32[]{:S(2)}, u32[]{:S(2)}) collective-permute-start(bf16[64,4096]{1,0:T(8,128)(2,1)} %bitcast.23), channel_id=1, source_target_pairs={{0,16},{1,49},{2,18},{3,51},{4,20},{5,53},{6,22},{7,55},{8,24},{9,... | collective-permute-start | bytes 1572872 | tf_op jit(solution)/shard_map/ppermute | solution.py:33
  1.5 16.8 %collective-permute-start.4 = (bf16[64,4096]{1,0:T(8,128)(2,1)}, bf16[64,4096]{1,0:T(8,128)(2,1)S(1)}, u32[]{:S(2)}, u32[]{:S(2)}) collective-permute-start(bf16[64,4096]{1,0:T(8,128)(2,1)} %bitcast.24), channel_id=1, source_target_pairs={{0,64},{1,193},{2,66},{3,195},{4,68},{5,197},{6,70},{7,199},{8,72}... | collective-permute-start | bytes 1572872 | tf_op jit(solution)/shard_map/ppermute | solution.py:33
  4.8 19.5 %collective-permute-start.2 = (bf16[64,4096]{1,0:T(8,128)(2,1)}, bf16[64,4096]{1,0:T(8,128)(2,1)S(1)}, u32[]{:S(2)}, u32[]{:S(2)}) collective-permute-start(bf16[64,4096]{1,0:T(8,128)(2,1)} %bitcast.25), channel_id=1, source_target_pairs={{0,48},{1,17},{2,50},{3,19},{4,52},{5,21},{6,54},{7,23},{8,56},{9,... | collective-permute-start | bytes 1572872 | tf_op jit(solution)/shard_map/ppermute | solution.py:33
  17.2 10.5 %collective-permute-start.1 = (bf16[64,4096]{1,0:T(8,128)(2,1)S(1)}, bf16[64,4096]{1,0:T(8,128)(2,1)}, u32[]{:S(2)}, u32[]{:S(2)}) collective-permute-start(bf16[64,4096]{1,0:T(8,128)(2,1)S(1)} %collective-permute-done.refs_2_), channel_id=1, source_target_pairs={{0,16},{1,49},{2,18},{3,51},{4,20},{5,53},{6,22},{7,55},{8,24},{9,... | collective-permute-start | bytes 1572872 | tf_op jit(solution)/shard_map/ppermute | solution.py:33
  18.3 18.2 %collective-permute-start.9 = (bf16[64,4096]{1,0:T(8,128)(2,1)S(1)}, bf16[64,4096]{1,0:T(8,128)(2,1)S(1)}, u32[]{:S(2)}, u32[]{:S(2)}) collective-permute-start(bf16[64,4096]{1,0:T(8,128)(2,1)S(1)} %collective-permute-done.4.refs_0_), channel_id=1, source_target_pairs={{0,64},{1,193},{2,66},{3,195},{4,68},{5,197},{6,70},{7,199},{8,72}... | collective-permute-start | bytes 1572872 | tf_op jit(solution)/shard_map/ppermute | solution.py:33
  22.8 15.2 %collective-permute-start.5 = (bf16[64,4096]{1,0:T(8,128)(2,1)S(1)}, bf16[64,4096]{1,0:T(8,128)(2,1)S(1)}, u32[]{:S(2)}, u32[]{:S(2)}) collective-permute-start(bf16[64,4096]{1,0:T(8,128)(2,1)S(1)} %collective-permute-done.4.refs_0_), channel_id=1, source_target_pairs={{0,16},{1,49},{2,18},{3,51},{4,20},{5,53},{6,22},{7,55},{8,24},{9,... | collective-permute-start | bytes 1572872 | tf_op jit(solution)/shard_map/ppermute | solution.py:33
  25.2 28.9 %collective-permute-start.7 = (bf16[64,4096]{1,0:T(8,128)(2,1)S(1)}, bf16[64,4096]{1,0:T(8,128)(2,1)}, u32[]{:S(2)}, u32[]{:S(2)}) collective-permute-start(bf16[64,4096]{1,0:T(8,128)(2,1)S(1)} %collective-permute-done.4.refs_0_), channel_id=1, source_target_pairs={{0,48},{1,17},{2,50},{3,19},{4,52},{5,21},{6,54},{7,23},{8,56},{9,... | collective-permute-start | bytes 1572872 | tf_op jit(solution)/shard_map/ppermute | solution.py:33
  36.6 17.5 %collective-permute-start.10 = (bf16[64,4096]{1,0:T(8,128)(2,1)S(1)}, bf16[64,4096]{1,0:T(8,128)(2,1)}, u32[]{:S(2)}, u32[]{:S(2)}) collective-permute-start(bf16[64,4096]{1,0:T(8,128)(2,1)S(1)} %collective-permute-done.9.refs_0_), channel_id=1, source_target_pairs={{0,16},{1,49},{2,18},{3,51},{4,20},{5,53},{6,22},{7,55},{8,24},{9,... | collective-permute-start | bytes 1572872 | tf_op jit(solution)/shard_map/ppermute | solution.py:33
  38.1 20.2 %collective-permute-start.6 = (bf16[64,4096]{1,0:T(8,128)(2,1)S(1)}, bf16[64,4096]{1,0:T(8,128)(2,1)}, u32[]{:S(2)}, u32[]{:S(2)}) collective-permute-start(bf16[64,4096]{1,0:T(8,128)(2,1)S(1)} %collective-permute-done.5.refs_2_), channel_id=1, source_target_pairs={{0,16},{1,49},{2,18},{3,51},{4,20},{5,53},{6,22},{7,55},{8,24},{9,... | collective-permute-start | bytes 1572872 | tf_op jit(solution)/shard_map/ppermute | solution.py:33
  39.2 19.4 %collective-permute-start.12 = (bf16[64,4096]{1,0:T(8,128)(2,1)S(1)}, bf16[64,4096]{1,0:T(8,128)(2,1)}, u32[]{:S(2)}, u32[]{:S(2)}) collective-permute-start(bf16[64,4096]{1,0:T(8,128)(2,1)S(1)} %collective-permute-done.9.refs_0_), channel_id=1, source_target_pairs={{0,48},{1,17},{2,50},{3,19},{4,52},{5,21},{6,54},{7,23},{8,56},{9,... | collective-permute-start | bytes 1572872 | tf_op jit(solution)/shard_map/ppermute | solution.py:33
  41.3 20.1 %collective-permute-start.14 = (bf16[64,4096]{1,0:T(8,128)(2,1)S(1)}, bf16[64,4096]{1,0:T(8,128)(2,1)}, u32[]{:S(2)}, u32[]{:S(2)}) collective-permute-start(bf16[64,4096]{1,0:T(8,128)(2,1)S(1)} %bitcast.26), channel_id=1, source_target_pairs={{0,192},{1,65},{2,194},{3,67},{4,196},{5,69},{6,198},{7,71},{8,200... | collective-permute-start | bytes 1572872 | tf_op jit(solution)/shard_map/ppermute | solution.py:33
  58.3 16.2 %collective-permute-start.11 = (bf16[64,4096]{1,0:T(8,128)(2,1)}, bf16[64,4096]{1,0:T(8,128)(2,1)S(1)}, u32[]{:S(2)}, u32[]{:S(2)}) collective-permute-start(bf16[64,4096]{1,0:T(8,128)(2,1)} %collective-permute-done.10.refs_2_), channel_id=1, source_target_pairs={{0,16},{1,49},{2,18},{3,51},{4,20},{5,53},{6,22},{7,55},{8,24},{9,... | collective-permute-start | bytes 1572872 | tf_op jit(solution)/shard_map/ppermute | solution.py:33
  61.4 17.4 %collective-permute-start.17 = (bf16[64,4096]{1,0:T(8,128)(2,1)}, bf16[64,4096]{1,0:T(8,128)(2,1)S(1)}, u32[]{:S(2)}, u32[]{:S(2)}) collective-permute-start(bf16[64,4096]{1,0:T(8,128)(2,1)} %collective-permute-done.14.refs_0_), channel_id=1, source_target_pairs={{0,48},{1,17},{2,50},{3,19},{4,52},{5,21},{6,54},{7,23},{8,56},{9,... | collective-permute-start | bytes 1572872 | tf_op jit(solution)/shard_map/ppermute | solution.py:33
  61.5 18.6 %collective-permute-start.16 = (bf16[64,4096]{1,0:T(8,128)(2,1)}, bf16[64,4096]{1,0:T(8,128)(2,1)S(1)}, u32[]{:S(2)}, u32[]{:S(2)}) collective-permute-start(bf16[64,4096]{1,0:T(8,128)(2,1)} %collective-permute-done.14.refs_0_), channel_id=1, source_target_pairs={{0,16},{1,49},{2,18},{3,51},{4,20},{5,53},{6,22},{7,55},{8,24},{9,... | collective-permute-start | bytes 1572872 | tf_op jit(solution)/shard_map/ppermute | solution.py:33
  63.4 16.9 %collective-permute-start.15 = (bf16[64,4096]{1,0:T(8,128)(2,1)}, bf16[64,4096]{1,0:T(8,128)(2,1)S(1)}, u32[]{:S(2)}, u32[]{:S(2)}) collective-permute-start(bf16[64,4096]{1,0:T(8,128)(2,1)} %collective-permute-done.1.refs_1_), channel_id=1, source_target_pairs={{0,192},{1,65},{2,194},{3,67},{4,196},{5,69},{6,198},{7,71},{8,200... | collective-permute-start | bytes 1572872 | tf_op jit(solution)/shard_map/ppermute | solution.py:33
  64.5 23.4 %collective-permute-start.3 = (f32[128,1024]{1,0:T(8,128)S(1)}, f32[128,1024]{1,0:T(8,128)S(1)}, u32[]{:S(2)}, u32[]{:S(2)}) collective-permute-start(f32[128,1024]{1,0:T(8,128)S(1)} %get-tuple-element.47.refs_5_), channel_id=1, source_target_pairs={{0,1},{1,0},{2,3},{3,2},{4,5},{5,4},{6,7},{7,6},{8,9},{9,8},{10,11... | collective-permute-start | bytes 1572872 | tf_op jit(solution)/shard_map/ppermute | solution.py:53
  74.5 13.5 %collective-permute-start.8 = (f32[128,1024]{1,0:T(8,128)}, f32[128,1024]{1,0:T(8,128)S(1)}, u32[]{:S(2)}, u32[]{:S(2)}) collective-permute-start(f32[128,1024]{1,0:T(8,128)} %get-tuple-element.51.refs_5_), channel_id=1, source_target_pairs={{0,1},{1,0},{2,3},{3,2},{4,5},{5,4},{6,7},{7,6},{8,9},{9,8},{10,11... | collective-permute-start | bytes 1572872 | tf_op jit(solution)/shard_map/ppermute | solution.py:53
  93.0 7.9 %collective-permute-start.21 = (bf16[64,1024]{1,0:T(8,128)(2,1)S(1)}, bf16[64,1024]{1,0:T(8,128)(2,1)S(1)}, u32[]{:S(2)}, u32[]{:S(2)}) collective-permute-start(bf16[64,1024]{1,0:T(8,128)(2,1)S(1)} %get-tuple-element.66), channel_id=1, source_target_pairs={{0,6},{1,15},{2,4},{3,13},{4,10},{5,3},{6,8},{7,1},{8,14},{9,7},{1... | collective-permute-start | bytes 393224 | tf_op jit(solution)/shard_map/ppermute | solution.py:49
  94.0 11.7 %collective-permute-start.22 = (bf16[64,1024]{1,0:T(8,128)(2,1)S(1)}, bf16[64,1024]{1,0:T(8,128)(2,1)S(1)}, u32[]{:S(2)}, u32[]{:S(2)}) collective-permute-start(bf16[64,1024]{1,0:T(8,128)(2,1)S(1)} %get-tuple-element.67), channel_id=1, source_target_pairs={{0,8},{1,9},{2,10},{3,11},{4,12},{5,13},{6,14},{7,15},{8,0},{9,1},... | collective-permute-start | bytes 393224 | tf_op jit(solution)/shard_map/ppermute | solution.py:49
  96.0 9.8 %collective-permute-start.23 = (bf16[64,1024]{1,0:T(8,128)(2,1)S(1)}, bf16[64,1024]{1,0:T(8,128)(2,1)S(1)}, u32[]{:S(2)}, u32[]{:S(2)}) collective-permute-start(bf16[64,1024]{1,0:T(8,128)(2,1)S(1)} %get-tuple-element.68), channel_id=1, source_target_pairs={{0,10},{1,11},{2,8},{3,9},{4,14},{5,15},{6,12},{7,13},{8,2},{9,3},... | collective-permute-start | bytes 393224 | tf_op jit(solution)/shard_map/ppermute | solution.py:49
  97.7 9.6 %collective-permute-start.24 = (bf16[64,1024]{1,0:T(8,128)(2,1)S(1)}, bf16[64,1024]{1,0:T(8,128)(2,1)S(1)}, u32[]{:S(2)}, u32[]{:S(2)}) collective-permute-start(bf16[64,1024]{1,0:T(8,128)(2,1)S(1)} %get-tuple-element.69), channel_id=1, source_target_pairs={{0,12},{1,5},{2,14},{3,7},{4,0},{5,9},{6,2},{7,11},{8,4},{9,13},{1... | collective-permute-start | bytes 393224 | tf_op jit(solution)/shard_map/ppermute | solution.py:49
  109.6 9.1 %collective-permute-start.26 = (f32[4,64,128]{2,1,0:T(8,128)S(1)}, f32[4,64,128]{2,1,0:T(8,128)S(1)}, u32[]{:S(2)}, u32[]{:S(2)}) collective-permute-start(f32[4,64,128]{2,1,0:T(8,128)S(1)} %get-tuple-element.72), channel_id=1, source_target_pairs={{0,16},{16,32},{32,48},{48,0},{64,80},{80,96},{96,112},{112,64},{1... | collective-permute-start | bytes 393224 | tf_op jit(solution)/shard_map/ppermute | solution.py:23
  109.7 9.0 %collective-permute-start.27 = (f32[4,64,128]{2,1,0:T(8,128)S(1)}, f32[4,64,128]{2,1,0:T(8,128)S(1)}, u32[]{:S(2)}, u32[]{:S(2)}) collective-permute-start(f32[4,64,128]{2,1,0:T(8,128)S(1)} %get-tuple-element.73), channel_id=1, source_target_pairs={{0,32},{16,48},{32,0},{48,16},{64,96},{80,112},{96,64},{112,80},{1... | collective-permute-start | bytes 393224 | tf_op jit(solution)/shard_map/ppermute | solution.py:23
  119.3 9.6 %collective-permute-start.29 = (f32[64,128]{1,0:T(8,128)S(1)}, f32[64,128]{1,0:T(8,128)S(1)}, u32[]{:S(2)}, u32[]{:S(2)}) collective-permute-start(f32[64,128]{1,0:T(8,128)S(1)} %get-tuple-element.76), channel_id=1, source_target_pairs={{0,64},{16,80},{32,96},{48,112},{64,128},{80,144},{96,160},{112,17... | collective-permute-start | bytes 98312 | tf_op jit(solution)/shard_map/ppermute | solution.py:23
  (22 other events, 136.0 us)

commit v3 on v2

--- a/solution.py
+++ b/solution.py
@@ -12,7 +12,6 @@
 BF16 = jnp.bfloat16
 VMEM_LIMIT = 14 * 1024 * 1024
 WIDTH = 256
-TOKEN = jax.ShapeDtypeStruct((8, 128), F32)
 
 
 def pq_shift(value, dz, dx):
@@ -61,9 +60,8 @@
     return pl.CostEstimate(flops=flops, bytes_accessed=bytes_accessed, transcendentals=0)
 
 
-def mask_kernel(screen_ref, a_ref, out_ref, token_ref):
+def mask_kernel(screen_ref, a_ref, out_ref):
     at = pl.program_id(0)
-    token_ref[...] = jnp.zeros(token_ref.shape, F32)
     for col in range(a_ref.shape[1] // TILE):
         cols = slice(col * TILE, (col + 1) * TILE)
         for row in range(WIDTH // TILE):
@@ -76,15 +74,12 @@
     rows, cols = integrals.shape
     return pl.pallas_call(
         mask_kernel,
-        out_shape=[jax.ShapeDtypeStruct((rows // WIDTH, cols, WIDTH), BF16), TOKEN],
+        out_shape=jax.ShapeDtypeStruct((rows // WIDTH, cols, WIDTH), BF16),
         grid_spec=pltpu.PrefetchScalarGridSpec(
             num_scalar_prefetch=1,
             grid=(rows // WIDTH,),
             in_specs=[pl.BlockSpec((WIDTH, cols), lambda at, _: (at, 0))],
-            out_specs=[
-                pl.BlockSpec((1, cols, WIDTH), lambda at, _: (at, 0, 0)),
-                pl.BlockSpec(TOKEN.shape, lambda at, _: (0, 0)),
-            ],
+            out_specs=pl.BlockSpec((1, cols, WIDTH), lambda at, _: (at, 0, 0)),
         ),
         compiler_params=params(),
         cost_estimate=cost(rows * cols, 4 * rows * cols),
@@ -237,20 +232,17 @@
     block[0, -1] = send(own, 0, 1)
     block[-1, 0] = send(own, 1, 0)
     block[0, 1] = send(own, 0, -1)
-    masked, token = mask(
+    masked = mask(
         integrals.reshape(slabs * pq_rows, rs_cols),
         screen.reshape(slabs * (pq_rows // TILE), rs_cols // TILE),
     )
-    x_less, token = lax.optimization_barrier((block[0, -1], token))
-    block[0, 2] = send(x_less, 0, 1)
+    block[0, 2] = send(block[0, -1], 0, 1)
     block[2, 0] = send(block[-1, 0], 1, 0)
     block[-1, -1] = send(after(block[-1, 0], block[0, -1]), 0, 1)
     block[-1, 1] = send(after(block[-1, 0], block[0, 1]), 0, -1)
     block[-1, 2] = send(block[-1, -1], 0, 1)
     block[1, 0] = send(after(own, block[0, 2]), -1, 0)
-    first = half_transform(
-        swap_at, masked, [own, block[0, 2]], [block[0, -1], block[0, 1]], [token]
-    )
+    first = half_transform(swap_at, masked, [own, block[0, 2]], [block[0, -1], block[0, 1]])
     block[2, -1] = send(after(block[2, 0], block[0, 2]), 0, 1)
     block[2, 1] = send(after(block[2, 0], block[-1, -1]), 0, -1)
     block[2, 2] = send(after(block[2, -1], block[-1, 2], block[-1, 1], *first), 0, 1)

time: 134 us -> 132 us (0.985)
  starting transfers between devices: 50 us -> 57 us
  local copies, waits for them, and re-layouts: 18.1 us -> 12.1 us
  waiting for transfers between devices: 40.8 us -> 37.8 us
    unnamed x28 -> x34, local copies, waits for them, and re-layouts: 17.9 us -> 12 us
    ppermute x6, waiting for transfers between devices: 10.5 us -> 6.1 us  [pq_shift(): return lax.ppermute(value, 'pq', perm)]
    ppermute x6, starting transfers between devices: 12.9 us -> 16.9 us  [pq_shift(): return lax.ppermute(value, 'pq', perm)]
    ppermute x15, starting transfers between devices: 26.6 us -> 29.5 us  [send(): return lax.ppermute(value, ('pq', 'rs'), perm)]
    ppermute x15, waiting for transfers between devices: 23.7 us -> 25.1 us  [send(): return lax.ppermute(value, ('pq', 'rs'), perm)]
  transfers between devices with their start and end apart: 32 -> 32, of which waited for: 13 -> 12; matrix products, arithmetic and copies ran while one was open for 0% -> 0% of each run, Pallas kernels for 15% -> 14%
where the time goes in v3:
time: 132 us; the launch traced here: 131 us
  starting transfers between devices  57 us (43%)
  waiting for transfers between devices  37.8 us (29%)
  Pallas kernels  21.5 us (16%)
  local copies, waits for them, and re-layouts  12.1 us (9%)
  between operations  2.2 us (2%)
    ppermute x15, starting transfers between devices, send(): return lax.ppermute(value, ('pq', 'rs'), perm)  29.5 us
    ppermute x15, waiting for transfers between devices, send(): return lax.ppermute(value, ('pq', 'rs'), perm)  25.1 us
    ppermute x6, starting transfers between devices, pq_shift(): return lax.ppermute(value, 'pq', perm)  16.9 us
    pallas_call x4, Pallas kernels, half_transform(): pl.pallas_call(half_kernel, out_shape=[out, out], in_specs=[pl.BlockSpec(...  15.1 us
    unnamed x34, local copies, waits for them, and re-layouts  12 us
    ppermute x7, starting transfers between devices, rs_send(): return lax.ppermute(value, 'rs', perm)  10 us
    ppermute x7, waiting for transfers between devices, rs_send(): return lax.ppermute(value, 'rs', perm)  6.31 us
    ppermute x6, waiting for transfers between devices, pq_shift(): return lax.ppermute(value, 'pq', perm)  6.1 us
  transfers between devices with their start and end apart: 32, of which 12 were waited for; matrix products, arithmetic and copies ran while one was open for 0% of the time, Pallas kernels for 14%

profile of v3, /device:TPU:16, one launch (start us, length us, event | category | flops | bytes accessed | tf_op | source)
XLA Modules:
  0.0 130.6 jit_solution(4159693644772798928)
XLA Ops:
  1.5 3.3 %collective-permute-start.4 = (bf16[64,4096]{1,0:T(8,128)(2,1)}, bf16[64,4096]{1,0:T(8,128)(2,1)S(1)}, u32[]{:S(2)}, u32[]{:S(2)}) collective-permute-start(bf16[64,4096]{1,0:T(8,128)(2,1)} %bitcast.24), channel_id=1, source_target_pairs={{0,64},{1,193},{2,66},{3,195},{4,68},{5,197},{6,70},{7,199},{8,72}... | collective-permute-start | bytes 1572872 | tf_op jit(solution)/shard_map/ppermute | solution.py:32
  6.5 4.1 %collective-permute-done.refs_2_ = bf16[64,4096]{1,0:T(8,128)(2,1)S(1)} collective-permute-done((bf16[64,4096]{1,0:T(8,128)(2,1)}, bf16[64,4096]{1,0:T(8,128)(2,1)S(1)}, u32[]{:S(2)}, u32[]{:S(2)}) %collective-permute-start) | collective-permute-done | bytes 524320 | tf_op jit(solution)/shard_map/ppermute | solution.py:32
  11.7 5.5 %collective-permute-done.4.refs_0_ = bf16[64,4096]{1,0:T(8,128)(2,1)S(1)} collective-permute-done((bf16[64,4096]{1,0:T(8,128)(2,1)}, bf16[64,4096]{1,0:T(8,128)(2,1)S(1)}, u32[]{:S(2)}, u32[]{:S(2)}) %collective-permute-start.4) | collective-permute-done | bytes 524320 | tf_op jit(solution)/shard_map/ppermute | solution.py:32
  17.1 4.6 %collective-permute-start.9 = (bf16[64,4096]{1,0:T(8,128)(2,1)S(1)}, bf16[64,4096]{1,0:T(8,128)(2,1)S(1)}, u32[]{:S(2)}, u32[]{:S(2)}) collective-permute-start(bf16[64,4096]{1,0:T(8,128)(2,1)S(1)} %collective-permute-done.4.refs_0_), channel_id=1, source_target_pairs={{0,64},{1,193},{2,66},{3,195},{4,68},{5,197},{6,70},{7,199},{8,72}... | collective-permute-start | bytes 1572872 | tf_op jit(solution)/shard_map/ppermute | solution.py:32
  25.8 10.7 %collective-permute-done.9.refs_0_ = bf16[64,4096]{1,0:T(8,128)(2,1)S(1)} collective-permute-done((bf16[64,4096]{1,0:T(8,128)(2,1)S(1)}, bf16[64,4096]{1,0:T(8,128)(2,1)S(1)}, u32[]{:S(2)}, u32[]{:S(2)}) %collective-permute-start.9) | collective-permute-done | bytes 524320 | tf_op jit(solution)/shard_map/ppermute | solution.py:32
  39.2 2.1 %collective-permute-start.12 = (bf16[64,4096]{1,0:T(8,128)(2,1)S(1)}, bf16[64,4096]{1,0:T(8,128)(2,1)}, u32[]{:S(2)}, u32[]{:S(2)}) collective-permute-start(bf16[64,4096]{1,0:T(8,128)(2,1)S(1)} %collective-permute-done.9.refs_0_), channel_id=1, source_target_pairs={{0,48},{1,17},{2,50},{3,19},{4,52},{5,21},{6,54},{7,23},{8,56},{9,... | collective-permute-start | bytes 1572872 | tf_op jit(solution)/shard_map/ppermute | solution.py:32
  41.3 3.9 %collective-permute-start.14 = (bf16[64,4096]{1,0:T(8,128)(2,1)}, bf16[64,4096]{1,0:T(8,128)(2,1)}, u32[]{:S(2)}, u32[]{:S(2)}) collective-permute-start(bf16[64,4096]{1,0:T(8,128)(2,1)} %bitcast.26), channel_id=1, source_target_pairs={{0,192},{1,65},{2,194},{3,67},{4,196},{5,69},{6,198},{7,71},{8,200... | collective-permute-start | bytes 1572872 | tf_op jit(solution)/shard_map/ppermute | solution.py:32
  45.2 3.4 %copy-done = bf16[2,512,4096]{2,1,0:T(8,128)(2,1)S(1)} copy-done((bf16[2,512,4096]{2,1,0:T(8,128)(2,1)S(1)}, bf16[2,512,4096]{2,1,0:T(8,128)(2,1)}, u32[]{:S(2)}) %copy-start) | copy-done | bytes 8388632
  49.3 3.3 %shard_map.46.a_ref = bf16[4,4096,256]{2,1,0:T(8,128)(2,1)S(1)} custom-call(s32[8,32]{1,0:T(8,128)S(1)} %bitcast.28, bf16[1024,4096]{1,0:T(8,128)(2,1)S(1)} %bitcast.22), custom_call_target="tpu_custom_call" | custom-call | flops 4194304 | bytes 16777216 | tf_op jit(solution)/shard_map/pallas_call | solution.py:75
  53.7 2.3 %shard_map.47 = (f32[128,1024]{1,0:T(8,128)S(1)}, f32[128,1024]{1,0:T(8,128)S(1)}) custom-call(s32[1]{0:T(128)} %bitcast.18.swap_ref, bf16[4,4096,256]{2,1,0:T(8,128)(2,1)S(1)} %shard_map.46.a_ref, bf16[64,4096]{1,0:T(8,128)(2,1)S(1)} %bitcast.27, bf16[64,4096]{1,0:T(8,128)(2,1)S(1)} %copy-done.10, bf16[64,4096]{1,0:T(8,128)(2,1)S(1)} %copy-done.13, ...), custom_call_target="tpu_custom_call" | custom-call | flops 2147483648 | bytes 11534336 | tf_op jit(solution)/shard_map/pallas_call | solution.py:108
  58.6 3.0 %collective-permute-start.17 = (bf16[64,4096]{1,0:T(8,128)(2,1)}, bf16[64,4096]{1,0:T(8,128)(2,1)S(1)}, u32[]{:S(2)}, u32[]{:S(2)}) collective-permute-start(bf16[64,4096]{1,0:T(8,128)(2,1)} %collective-permute-done.14.refs_0_), channel_id=1, source_target_pairs={{0,48},{1,17},{2,50},{3,19},{4,52},{5,21},{6,54},{7,23},{8,56},{9,... | collective-permute-start | bytes 1572872 | tf_op jit(solution)/shard_map/ppermute | solution.py:32
  61.6 3.0 %collective-permute-start.15 = (bf16[64,4096]{1,0:T(8,128)(2,1)S(1)}, bf16[64,4096]{1,0:T(8,128)(2,1)S(1)}, u32[]{:S(2)}, u32[]{:S(2)}) collective-permute-start(bf16[64,4096]{1,0:T(8,128)(2,1)S(1)} %copy-done.11), channel_id=1, source_target_pairs={{0,192},{1,65},{2,194},{3,67},{4,196},{5,69},{6,198},{7,71},{8,200... | collective-permute-start | bytes 1572872 | tf_op jit(solution)/shard_map/ppermute | solution.py:32
  65.6 4.2 %shard_map.48 = (f32[128,1024]{1,0:T(8,128)S(1)}, f32[128,1024]{1,0:T(8,128)}) custom-call(s32[1]{0:T(128)} %bitcast.18.swap_ref, bf16[4,4096,256]{2,1,0:T(8,128)(2,1)S(1)} %shard_map.46.a_ref, bf16[64,4096]{1,0:T(8,128)(2,1)S(1)} %collective-permute-done.4.refs_0_, bf16[64,4096]{1,0:T(8,128)(2,1)} %collective-permute-done.6.refs_1_, ...), custom_call_target="tpu_custom_call" | custom-call | flops 2147483648 | bytes 11534336 | tf_op jit(solution)/shard_map/pallas_call | solution.py:108
  69.8 2.1 %collective-permute-done.11.refs_1_ = bf16[64,4096]{1,0:T(8,128)(2,1)S(1)} collective-permute-done((bf16[64,4096]{1,0:T(8,128)(2,1)}, bf16[64,4096]{1,0:T(8,128)(2,1)S(1)}, u32[]{:S(2)}, u32[]{:S(2)}) %collective-permute-start.11) | collective-permute-done | bytes 524320 | tf_op jit(solution)/shard_map/ppermute | solution.py:32
  71.9 4.3 %shard_map.49 = (f32[128,1024]{1,0:T(8,128)S(1)}, f32[128,1024]{1,0:T(8,128)}) custom-call(s32[1]{0:T(128)} %bitcast.18.swap_ref, bf16[4,4096,256]{2,1,0:T(8,128)(2,1)S(1)} %shard_map.46.a_ref, bf16[64,4096]{1,0:T(8,128)(2,1)S(1)} %copy-done.5, bf16[64,4096]{1,0:T(8,128)(2,1)S(1)} %collective-permute-done.11.refs_1_, ...), custom_call_target="tpu_custom_call" | custom-call | flops 2147483648 | bytes 11534336 | tf_op jit(solution)/shard_map/pallas_call | solution.py:108
  77.5 4.2 %shard_map.50 = (f32[128,1024]{1,0:T(8,128)S(1)}, f32[128,1024]{1,0:T(8,128)}) custom-call(s32[1]{0:T(128)} %bitcast.18.swap_ref, bf16[4,4096,256]{2,1,0:T(8,128)(2,1)S(1)} %shard_map.46.a_ref, bf16[64,4096]{1,0:T(8,128)(2,1)} %collective-permute-done.14.refs_0_, bf16[64,4096]{1,0:T(8,128)(2,1)S(1)} %collective-permute-done.15.refs_1_, ...), custom_call_target="tpu_custom_call" | custom-call | flops 2147483648 | bytes 11534336 | tf_op jit(solution)/shard_map/pallas_call | solution.py:108
  91.3 2.0 %collective-permute-start.22 = (bf16[64,1024]{1,0:T(8,128)(2,1)S(1)}, bf16[64,1024]{1,0:T(8,128)(2,1)S(1)}, u32[]{:S(2)}, u32[]{:S(2)}) collective-permute-start(bf16[64,1024]{1,0:T(8,128)(2,1)S(1)} %get-tuple-element.59), channel_id=1, source_target_pairs={{0,8},{1,9},{2,10},{3,11},{4,12},{5,13},{6,14},{7,15},{8,0},{9,1},... | collective-permute-start | bytes 393224 | tf_op jit(solution)/shard_map/ppermute | solution.py:48
  98.2 4.8 %collective-permute-done.22.refs_4_ = bf16[64,1024]{1,0:T(8,128)(2,1)S(1)} collective-permute-done((bf16[64,1024]{1,0:T(8,128)(2,1)S(1)}, bf16[64,1024]{1,0:T(8,128)(2,1)S(1)}, u32[]{:S(2)}, u32[]{:S(2)}) %collective-permute-start.22) | collective-permute-done | bytes 131104 | tf_op jit(solution)/shard_map/ppermute | solution.py:48
  106.8 3.1 %collective-permute-start.26 = (f32[4,64,128]{2,1,0:T(8,128)S(1)}, f32[4,64,128]{2,1,0:T(8,128)S(1)}, u32[]{:S(2)}, u32[]{:S(2)}) collective-permute-start(f32[4,64,128]{2,1,0:T(8,128)S(1)} %get-tuple-element.64), channel_id=1, source_target_pairs={{0,16},{16,32},{32,48},{48,0},{64,80},{80,96},{96,112},{112,64},{1... | collective-permute-start | bytes 393224 | tf_op jit(solution)/shard_map/ppermute | solution.py:22
  110.9 2.5 %collective-permute-start.28 = (f32[4,64,128]{2,1,0:T(8,128)S(1)}, f32[4,64,128]{2,1,0:T(8,128)S(1)}, u32[]{:S(2)}, u32[]{:S(2)}) collective-permute-start(f32[4,64,128]{2,1,0:T(8,128)S(1)} %get-tuple-element.66), channel_id=1, source_target_pairs={{0,48},{16,0},{32,16},{48,32},{64,112},{80,64},{96,80},{112,96},{1... | collective-permute-start | bytes 393224 | tf_op jit(solution)/shard_map/ppermute | solution.py:22
  113.6 3.1 %collective-permute-done.27.c_ref = f32[4,64,128]{2,1,0:T(8,128)S(1)} collective-permute-done((f32[4,64,128]{2,1,0:T(8,128)S(1)}, f32[4,64,128]{2,1,0:T(8,128)S(1)}, u32[]{:S(2)}, u32[]{:S(2)}) %collective-permute-start.27) | collective-permute-done | bytes 131104 | tf_op jit(solution)/shard_map/ppermute | solution.py:22
  116.8 5.3 %collective-permute-start.29 = (f32[64,128]{1,0:T(8,128)S(1)}, f32[64,128]{1,0:T(8,128)S(1)}, u32[]{:S(2)}, u32[]{:S(2)}) collective-permute-start(f32[64,128]{1,0:T(8,128)S(1)} %get-tuple-element.68), channel_id=1, source_target_pairs={{0,64},{16,80},{32,96},{48,112},{64,128},{80,144},{96,160},{112,17... | collective-permute-start | bytes 98312 | tf_op jit(solution)/shard_map/ppermute | solution.py:22
  123.2 3.9 %collective-permute-start.31 = (f32[64,128]{1,0:T(8,128)S(1)}, f32[64,128]{1,0:T(8,128)S(1)}, u32[]{:S(2)}, u32[]{:S(2)}) collective-permute-start(f32[64,128]{1,0:T(8,128)S(1)} %get-tuple-element.70), channel_id=1, source_target_pairs={{0,192},{16,208},{32,224},{48,240},{64,0},{80,16},{96,32},{112,48}... | collective-permute-start | bytes 98312 | tf_op jit(solution)/shard_map/ppermute | solution.py:22
  127.1 2.8 %collective-permute-done.30.c_ref = f32[64,128]{1,0:T(8,128)S(1)} collective-permute-done((f32[64,128]{1,0:T(8,128)S(1)}, f32[64,128]{1,0:T(8,128)S(1)}, u32[]{:S(2)}, u32[]{:S(2)}) %collective-permute-start.30) | collective-permute-done | bytes 32800 | tf_op jit(solution)/shard_map/ppermute | solution.py:22
  (85 shorter events, 36.9 us)
Async XLA Ops:
  0.0 10.6 %collective-permute-start = (bf16[64,4096]{1,0:T(8,128)(2,1)}, bf16[64,4096]{1,0:T(8,128)(2,1)S(1)}, u32[]{:S(2)}, u32[]{:S(2)}) collective-permute-start(bf16[64,4096]{1,0:T(8,128)(2,1)} %bitcast.23), channel_id=1, source_target_pairs={{0,16},{1,49},{2,18},{3,51},{4,20},{5,53},{6,22},{7,55},{8,24},{9,... | collective-permute-start | bytes 1572872 | tf_op jit(solution)/shard_map/ppermute | solution.py:32
  1.5 15.7 %collective-permute-start.4 = (bf16[64,4096]{1,0:T(8,128)(2,1)}, bf16[64,4096]{1,0:T(8,128)(2,1)S(1)}, u32[]{:S(2)}, u32[]{:S(2)}) collective-permute-start(bf16[64,4096]{1,0:T(8,128)(2,1)} %bitcast.24), channel_id=1, source_target_pairs={{0,64},{1,193},{2,66},{3,195},{4,68},{5,197},{6,70},{7,199},{8,72}... | collective-permute-start | bytes 1572872 | tf_op jit(solution)/shard_map/ppermute | solution.py:32
  4.8 18.5 %collective-permute-start.2 = (bf16[64,4096]{1,0:T(8,128)(2,1)}, bf16[64,4096]{1,0:T(8,128)(2,1)S(1)}, u32[]{:S(2)}, u32[]{:S(2)}) collective-permute-start(bf16[64,4096]{1,0:T(8,128)(2,1)} %bitcast.25), channel_id=1, source_target_pairs={{0,48},{1,17},{2,50},{3,19},{4,52},{5,21},{6,54},{7,23},{8,56},{9,... | collective-permute-start | bytes 1572872 | tf_op jit(solution)/shard_map/ppermute | solution.py:32
  10.6 15.2 %collective-permute-start.1 = (bf16[64,4096]{1,0:T(8,128)(2,1)S(1)}, bf16[64,4096]{1,0:T(8,128)(2,1)S(1)}, u32[]{:S(2)}, u32[]{:S(2)}) collective-permute-start(bf16[64,4096]{1,0:T(8,128)(2,1)S(1)} %collective-permute-done.refs_2_), channel_id=1, source_target_pairs={{0,16},{1,49},{2,18},{3,51},{4,20},{5,53},{6,22},{7,55},{8,24},{9,... | collective-permute-start | bytes 1572872 | tf_op jit(solution)/shard_map/ppermute | solution.py:32
  17.1 19.4 %collective-permute-start.9 = (bf16[64,4096]{1,0:T(8,128)(2,1)S(1)}, bf16[64,4096]{1,0:T(8,128)(2,1)S(1)}, u32[]{:S(2)}, u32[]{:S(2)}) collective-permute-start(bf16[64,4096]{1,0:T(8,128)(2,1)S(1)} %collective-permute-done.4.refs_0_), channel_id=1, source_target_pairs={{0,64},{1,193},{2,66},{3,195},{4,68},{5,197},{6,70},{7,199},{8,72}... | collective-permute-start | bytes 1572872 | tf_op jit(solution)/shard_map/ppermute | solution.py:32
  21.8 16.3 %collective-permute-start.5 = (bf16[64,4096]{1,0:T(8,128)(2,1)S(1)}, bf16[64,4096]{1,0:T(8,128)(2,1)S(1)}, u32[]{:S(2)}, u32[]{:S(2)}) collective-permute-start(bf16[64,4096]{1,0:T(8,128)(2,1)S(1)} %collective-permute-done.4.refs_0_), channel_id=1, source_target_pairs={{0,16},{1,49},{2,18},{3,51},{4,20},{5,53},{6,22},{7,55},{8,24},{9,... | collective-permute-start | bytes 1572872 | tf_op jit(solution)/shard_map/ppermute | solution.py:32
  24.1 32.0 %collective-permute-start.7 = (bf16[64,4096]{1,0:T(8,128)(2,1)S(1)}, bf16[64,4096]{1,0:T(8,128)(2,1)S(1)}, u32[]{:S(2)}, u32[]{:S(2)}) collective-permute-start(bf16[64,4096]{1,0:T(8,128)(2,1)S(1)} %collective-permute-done.4.refs_0_), channel_id=1, source_target_pairs={{0,48},{1,17},{2,50},{3,19},{4,52},{5,21},{6,54},{7,23},{8,56},{9,... | collective-permute-start | bytes 1572872 | tf_op jit(solution)/shard_map/ppermute | solution.py:32
  36.6 20.3 %collective-permute-start.10 = (bf16[64,4096]{1,0:T(8,128)(2,1)S(1)}, bf16[64,4096]{1,0:T(8,128)(2,1)}, u32[]{:S(2)}, u32[]{:S(2)}) collective-permute-start(bf16[64,4096]{1,0:T(8,128)(2,1)S(1)} %collective-permute-done.9.refs_0_), channel_id=1, source_target_pairs={{0,16},{1,49},{2,18},{3,51},{4,20},{5,53},{6,22},{7,55},{8,24},{9,... | collective-permute-start | bytes 1572872 | tf_op jit(solution)/shard_map/ppermute | solution.py:32
  38.1 20.2 %collective-permute-start.6 = (bf16[64,4096]{1,0:T(8,128)(2,1)S(1)}, bf16[64,4096]{1,0:T(8,128)(2,1)}, u32[]{:S(2)}, u32[]{:S(2)}) collective-permute-start(bf16[64,4096]{1,0:T(8,128)(2,1)S(1)} %collective-permute-done.5.refs_2_), channel_id=1, source_target_pairs={{0,16},{1,49},{2,18},{3,51},{4,20},{5,53},{6,22},{7,55},{8,24},{9,... | collective-permute-start | bytes 1572872 | tf_op jit(solution)/shard_map/ppermute | solution.py:32
  39.2 19.4 %collective-permute-start.12 = (bf16[64,4096]{1,0:T(8,128)(2,1)S(1)}, bf16[64,4096]{1,0:T(8,128)(2,1)}, u32[]{:S(2)}, u32[]{:S(2)}) collective-permute-start(bf16[64,4096]{1,0:T(8,128)(2,1)S(1)} %collective-permute-done.9.refs_0_), channel_id=1, source_target_pairs={{0,48},{1,17},{2,50},{3,19},{4,52},{5,21},{6,54},{7,23},{8,56},{9,... | collective-permute-start | bytes 1572872 | tf_op jit(solution)/shard_map/ppermute | solution.py:32
  41.3 17.3 %collective-permute-start.14 = (bf16[64,4096]{1,0:T(8,128)(2,1)}, bf16[64,4096]{1,0:T(8,128)(2,1)}, u32[]{:S(2)}, u32[]{:S(2)}) collective-permute-start(bf16[64,4096]{1,0:T(8,128)(2,1)} %bitcast.26), channel_id=1, source_target_pairs={{0,192},{1,65},{2,194},{3,67},{4,196},{5,69},{6,198},{7,71},{8,200... | collective-permute-start | bytes 1572872 | tf_op jit(solution)/shard_map/ppermute | solution.py:32
  58.3 13.6 %collective-permute-start.11 = (bf16[64,4096]{1,0:T(8,128)(2,1)}, bf16[64,4096]{1,0:T(8,128)(2,1)S(1)}, u32[]{:S(2)}, u32[]{:S(2)}) collective-permute-start(bf16[64,4096]{1,0:T(8,128)(2,1)} %collective-permute-done.10.refs_2_), channel_id=1, source_target_pairs={{0,16},{1,49},{2,18},{3,51},{4,20},{5,53},{6,22},{7,55},{8,24},{9,... | collective-permute-start | bytes 1572872 | tf_op jit(solution)/shard_map/ppermute | solution.py:32
  58.6 17.6 %collective-permute-start.17 = (bf16[64,4096]{1,0:T(8,128)(2,1)}, bf16[64,4096]{1,0:T(8,128)(2,1)S(1)}, u32[]{:S(2)}, u32[]{:S(2)}) collective-permute-start(bf16[64,4096]{1,0:T(8,128)(2,1)} %collective-permute-done.14.refs_0_), channel_id=1, source_target_pairs={{0,48},{1,17},{2,50},{3,19},{4,52},{5,21},{6,54},{7,23},{8,56},{9,... | collective-permute-start | bytes 1572872 | tf_op jit(solution)/shard_map/ppermute | solution.py:32
  61.5 15.9 %collective-permute-start.16 = (bf16[64,4096]{1,0:T(8,128)(2,1)}, bf16[64,4096]{1,0:T(8,128)(2,1)S(1)}, u32[]{:S(2)}, u32[]{:S(2)}) collective-permute-start(bf16[64,4096]{1,0:T(8,128)(2,1)} %collective-permute-done.14.refs_0_), channel_id=1, source_target_pairs={{0,16},{1,49},{2,18},{3,51},{4,20},{5,53},{6,22},{7,55},{8,24},{9,... | collective-permute-start | bytes 1572872 | tf_op jit(solution)/shard_map/ppermute | solution.py:32
  61.6 15.9 %collective-permute-start.15 = (bf16[64,4096]{1,0:T(8,128)(2,1)S(1)}, bf16[64,4096]{1,0:T(8,128)(2,1)S(1)}, u32[]{:S(2)}, u32[]{:S(2)}) collective-permute-start(bf16[64,4096]{1,0:T(8,128)(2,1)S(1)} %copy-done.11), channel_id=1, source_target_pairs={{0,192},{1,65},{2,194},{3,67},{4,196},{5,69},{6,198},{7,71},{8,200... | collective-permute-start | bytes 1572872 | tf_op jit(solution)/shard_map/ppermute | solution.py:32
  64.5 20.7 %collective-permute-start.3 = (f32[128,1024]{1,0:T(8,128)S(1)}, f32[128,1024]{1,0:T(8,128)S(1)}, u32[]{:S(2)}, u32[]{:S(2)}) collective-permute-start(f32[128,1024]{1,0:T(8,128)S(1)} %get-tuple-element.39.refs_5_), channel_id=1, source_target_pairs={{0,1},{1,0},{2,3},{3,2},{4,5},{5,4},{6,7},{7,6},{8,9},{9,8},{10,11... | collective-permute-start | bytes 1572872 | tf_op jit(solution)/shard_map/ppermute | solution.py:52
  71.9 13.3 %collective-permute-start.8 = (f32[128,1024]{1,0:T(8,128)}, f32[128,1024]{1,0:T(8,128)S(1)}, u32[]{:S(2)}, u32[]{:S(2)}) collective-permute-start(f32[128,1024]{1,0:T(8,128)} %get-tuple-element.43.refs_5_), channel_id=1, source_target_pairs={{0,1},{1,0},{2,3},{3,2},{4,5},{5,4},{6,7},{7,6},{8,9},{9,8},{10,11... | collective-permute-start | bytes 1572872 | tf_op jit(solution)/shard_map/ppermute | solution.py:52
  89.1 7.7 %collective-permute-start.20 = (bf16[64,1024]{1,0:T(8,128)(2,1)S(1)}, bf16[64,1024]{1,0:T(8,128)(2,1)S(1)}, u32[]{:S(2)}, u32[]{:S(2)}) collective-permute-start(bf16[64,1024]{1,0:T(8,128)(2,1)S(1)} %get-tuple-element.57), channel_id=1, source_target_pairs={{0,4},{1,13},{2,6},{3,15},{4,8},{5,1},{6,10},{7,3},{8,12},{9,5},{1... | collective-permute-start | bytes 393224 | tf_op jit(solution)/shard_map/ppermute | solution.py:48
  90.3 7.9 %collective-permute-start.21 = (bf16[64,1024]{1,0:T(8,128)(2,1)S(1)}, bf16[64,1024]{1,0:T(8,128)(2,1)S(1)}, u32[]{:S(2)}, u32[]{:S(2)}) collective-permute-start(bf16[64,1024]{1,0:T(8,128)(2,1)S(1)} %get-tuple-element.58), channel_id=1, source_target_pairs={{0,6},{1,15},{2,4},{3,13},{4,10},{5,3},{6,8},{7,1},{8,14},{9,7},{1... | collective-permute-start | bytes 393224 | tf_op jit(solution)/shard_map/ppermute | solution.py:48
  91.3 11.8 %collective-permute-start.22 = (bf16[64,1024]{1,0:T(8,128)(2,1)S(1)}, bf16[64,1024]{1,0:T(8,128)(2,1)S(1)}, u32[]{:S(2)}, u32[]{:S(2)}) collective-permute-start(bf16[64,1024]{1,0:T(8,128)(2,1)S(1)} %get-tuple-element.59), channel_id=1, source_target_pairs={{0,8},{1,9},{2,10},{3,11},{4,12},{5,13},{6,14},{7,15},{8,0},{9,1},... | collective-permute-start | bytes 393224 | tf_op jit(solution)/shard_map/ppermute | solution.py:48
  93.2 9.8 %collective-permute-start.23 = (bf16[64,1024]{1,0:T(8,128)(2,1)S(1)}, bf16[64,1024]{1,0:T(8,128)(2,1)S(1)}, u32[]{:S(2)}, u32[]{:S(2)}) collective-permute-start(bf16[64,1024]{1,0:T(8,128)(2,1)S(1)} %get-tuple-element.60), channel_id=1, source_target_pairs={{0,10},{1,11},{2,8},{3,9},{4,14},{5,15},{6,12},{7,13},{8,2},{9,3},... | collective-permute-start | bytes 393224 | tf_op jit(solution)/shard_map/ppermute | solution.py:48
  95.0 9.5 %collective-permute-start.24 = (bf16[64,1024]{1,0:T(8,128)(2,1)S(1)}, bf16[64,1024]{1,0:T(8,128)(2,1)S(1)}, u32[]{:S(2)}, u32[]{:S(2)}) collective-permute-start(bf16[64,1024]{1,0:T(8,128)(2,1)S(1)} %get-tuple-element.61), channel_id=1, source_target_pairs={{0,12},{1,5},{2,14},{3,7},{4,0},{5,9},{6,2},{7,11},{8,4},{9,13},{1... | collective-permute-start | bytes 393224 | tf_op jit(solution)/shard_map/ppermute | solution.py:48
  116.8 10.3 %collective-permute-start.29 = (f32[64,128]{1,0:T(8,128)S(1)}, f32[64,128]{1,0:T(8,128)S(1)}, u32[]{:S(2)}, u32[]{:S(2)}) collective-permute-start(f32[64,128]{1,0:T(8,128)S(1)} %get-tuple-element.68), channel_id=1, source_target_pairs={{0,64},{16,80},{32,96},{48,112},{64,128},{80,144},{96,160},{112,17... | collective-permute-start | bytes 98312 | tf_op jit(solution)/shard_map/ppermute | solution.py:22
  122.1 7.8 %collective-permute-start.30 = (f32[64,128]{1,0:T(8,128)S(1)}, f32[64,128]{1,0:T(8,128)S(1)}, u32[]{:S(2)}, u32[]{:S(2)}) collective-permute-start(f32[64,128]{1,0:T(8,128)S(1)} %get-tuple-element.69), channel_id=1, source_target_pairs={{0,128},{16,144},{32,160},{48,176},{64,192},{80,208},{96,224},{112... | collective-permute-start | bytes 98312 | tf_op jit(solution)/shard_map/ppermute | solution.py:22
  (25 other events, 135.0 us)

commit v4 on v3

--- a/solution.py
+++ b/solution.py
@@ -99,7 +99,7 @@
         send_ref[:, cols] = jnp.where(swap, even, odd)
 
 
-def half_transform(swap, masked, even, odd, waits=()):
+def half_transform(swap, masked, even, odd, waits=(), held=()):
     count, cols, width = masked.shape
     rows = count * width
     pieces = list(even) + list(odd)
@@ -110,11 +110,12 @@
         out_shape=[out, out],
         in_specs=[pl.BlockSpec(memory_space=pltpu.SMEM)]
         + [pl.BlockSpec(memory_space=pltpu.VMEM)] * (1 + len(pieces))
-        + [pl.BlockSpec(memory_space=pl.ANY)] * len(waits),
+        + [pl.BlockSpec(memory_space=pl.ANY)] * len(waits)
+        + [pl.BlockSpec(memory_space=pltpu.VMEM)] * len(held),
         out_specs=[pl.BlockSpec(memory_space=pltpu.VMEM)] * 2,
         compiler_params=params(),
         cost_estimate=cost(4 * n * rows * cols, 2 * rows * cols + 4 * n * cols + 8 * n * rows),
-    )(swap, masked, *pieces, *waits)
+    )(swap, masked, *pieces, *waits, *held)
 
 
 def pack_kernel(keep_at_ref, got_at_ref, *refs):
@@ -253,10 +254,10 @@
         swap_at, masked, [block[-1, 0], block[-1, 2]], [block[-1, -1], block[-1, 1]], first
     )
     third = half_transform(
-        swap_at, masked, [block[2, 0], block[2, 2]], [block[2, -1], block[2, 1]], second
+        swap_at, masked, [block[2, 0], block[2, 2]], [block[2, -1], block[2, 1]], second, [pq_coeff]
     )
     fourth = half_transform(
-        swap_at, masked, [block[1, 0], block[1, 2]], [block[1, -1], block[1, 1]], third
+        swap_at, masked, [block[1, 0], block[1, 2]], [block[1, -1], block[1, 1]], third, [pq_coeff]
     )
     halves = [first, second, third, fourth]
     places = [((dz, even), (dz, odd)) for dz in (0, -1, 2, 1) for even, odd in ((0, -1), (2, 1))]

time: 132 us -> 132 us (level); the launches traced: 131 us -> 132 us
  waiting for transfers between devices: 37.8 us -> 46.8 us
  starting transfers between devices: 57 us -> 51.3 us
  local copies, waits for them, and re-layouts: 12.1 us -> 8.74 us
  Pallas kernels: 21.5 us -> 23 us
    ppermute x6, starting transfers between devices: 16.9 us -> 11.9 us  [pq_shift(): return lax.ppermute(value, 'pq', perm)]
    ppermute x7, waiting for transfers between devices: 6.31 us -> 10.8 us  [rs_send(): return lax.ppermute(value, 'rs', perm)]
    unnamed x34 -> x28, local copies, waits for them, and re-layouts: 12 us -> 8.56 us
    ppermute x6, waiting for transfers between devices: 6.1 us -> 9.39 us  [pq_shift(): return lax.ppermute(value, 'pq', perm)]
    ppermute x15, waiting for transfers between devices: 25.1 us -> 26.5 us  [send(): return lax.ppermute(value, ('pq', 'rs'), perm)]
  transfers between devices with their start and end apart: 32 -> 32, of which waited for: 12 -> 13; matrix products, arithmetic and copies ran while one was open for 0% -> 0% of each run, Pallas kernels for 14% -> 15%
where the time goes in v4:
time: 132 us
  starting transfers between devices  51.3 us (39%)
  waiting for transfers between devices  46.8 us (35%)
  Pallas kernels  23 us (17%)
  local copies, waits for them, and re-layouts  8.74 us (7%)
  between operations  2.24 us (2%)
    ppermute x15, starting transfers between devices, send(): return lax.ppermute(value, ('pq', 'rs'), perm)  29.5 us
    ppermute x15, waiting for transfers between devices, send(): return lax.ppermute(value, ('pq', 'rs'), perm)  26.5 us
    pallas_call x4, Pallas kernels, half_transform(): pl.pallas_call(half_kernel, out_shape=[out, out], in_specs=[pl.BlockSpec(...  16.3 us
    ppermute x6, starting transfers between devices, pq_shift(): return lax.ppermute(value, 'pq', perm)  11.9 us
    ppermute x7, waiting for transfers between devices, rs_send(): return lax.ppermute(value, 'rs', perm)  10.8 us
    ppermute x6, waiting for transfers between devices, pq_shift(): return lax.ppermute(value, 'pq', perm)  9.39 us
    ppermute x7, starting transfers between devices, rs_send(): return lax.ppermute(value, 'rs', perm)  9.36 us
    unnamed x28, local copies, waits for them, and re-layouts  8.56 us
  transfers between devices with their start and end apart: 32, of which 13 were waited for; matrix products, arithmetic and copies ran while one was open for 0% of the time, Pallas kernels for 15%

profile of v4, /device:TPU:16, one launch (start us, length us, event | category | flops | bytes accessed | tf_op | source)
XLA Modules:
  0.0 132.1 jit_solution(16367337191863608470)
XLA Ops:
  1.5 3.3 %collective-permute-start.4 = (bf16[64,4096]{1,0:T(8,128)(2,1)}, bf16[64,4096]{1,0:T(8,128)(2,1)S(1)}, u32[]{:S(2)}, u32[]{:S(2)}) collective-permute-start(bf16[64,4096]{1,0:T(8,128)(2,1)} %bitcast.24), channel_id=1, source_target_pairs={{0,64},{1,193},{2,66},{3,195},{4,68},{5,197},{6,70},{7,199},{8,72}... | collective-permute-start | bytes 1572872 | tf_op jit(solution)/shard_map/ppermute | solution.py:32
  6.5 4.1 %collective-permute-done.refs_2_ = bf16[64,4096]{1,0:T(8,128)(2,1)S(1)} collective-permute-done((bf16[64,4096]{1,0:T(8,128)(2,1)}, bf16[64,4096]{1,0:T(8,128)(2,1)S(1)}, u32[]{:S(2)}, u32[]{:S(2)}) %collective-permute-start) | collective-permute-done | bytes 524320 | tf_op jit(solution)/shard_map/ppermute | solution.py:32
  11.7 5.5 %collective-permute-done.4.refs_0_ = bf16[64,4096]{1,0:T(8,128)(2,1)S(1)} collective-permute-done((bf16[64,4096]{1,0:T(8,128)(2,1)}, bf16[64,4096]{1,0:T(8,128)(2,1)S(1)}, u32[]{:S(2)}, u32[]{:S(2)}) %collective-permute-start.4) | collective-permute-done | bytes 524320 | tf_op jit(solution)/shard_map/ppermute | solution.py:32
  17.1 4.6 %collective-permute-start.9 = (bf16[64,4096]{1,0:T(8,128)(2,1)S(1)}, bf16[64,4096]{1,0:T(8,128)(2,1)}, u32[]{:S(2)}, u32[]{:S(2)}) collective-permute-start(bf16[64,4096]{1,0:T(8,128)(2,1)S(1)} %collective-permute-done.4.refs_0_), channel_id=1, source_target_pairs={{0,64},{1,193},{2,66},{3,195},{4,68},{5,197},{6,70},{7,199},{8,72}... | collective-permute-start | bytes 1572872 | tf_op jit(solution)/shard_map/ppermute | solution.py:32
  25.8 10.8 %collective-permute-done.9.refs_0_ = bf16[64,4096]{1,0:T(8,128)(2,1)} collective-permute-done((bf16[64,4096]{1,0:T(8,128)(2,1)S(1)}, bf16[64,4096]{1,0:T(8,128)(2,1)}, u32[]{:S(2)}, u32[]{:S(2)}) %collective-permute-start.9) | collective-permute-done | bytes 524320 | tf_op jit(solution)/shard_map/ppermute | solution.py:32
  39.3 2.1 %collective-permute-start.12 = (bf16[64,4096]{1,0:T(8,128)(2,1)}, bf16[64,4096]{1,0:T(8,128)(2,1)}, u32[]{:S(2)}, u32[]{:S(2)}) collective-permute-start(bf16[64,4096]{1,0:T(8,128)(2,1)} %collective-permute-done.9.refs_0_), channel_id=1, source_target_pairs={{0,48},{1,17},{2,50},{3,19},{4,52},{5,21},{6,54},{7,23},{8,56},{9,... | collective-permute-start | bytes 1572872 | tf_op jit(solution)/shard_map/ppermute | solution.py:32
  41.4 3.9 %collective-permute-start.14 = (bf16[64,4096]{1,0:T(8,128)(2,1)}, bf16[64,4096]{1,0:T(8,128)(2,1)}, u32[]{:S(2)}, u32[]{:S(2)}) collective-permute-start(bf16[64,4096]{1,0:T(8,128)(2,1)} %bitcast.26), channel_id=1, source_target_pairs={{0,192},{1,65},{2,194},{3,67},{4,196},{5,69},{6,198},{7,71},{8,200... | collective-permute-start | bytes 1572872 | tf_op jit(solution)/shard_map/ppermute | solution.py:32
  45.3 3.4 %copy-done.1 = bf16[2,512,4096]{2,1,0:T(8,128)(2,1)S(1)} copy-done((bf16[2,512,4096]{2,1,0:T(8,128)(2,1)S(1)}, bf16[2,512,4096]{2,1,0:T(8,128)(2,1)}, u32[]{:S(2)}) %copy-start.1) | copy-done | bytes 8388632
  49.4 3.3 %shard_map.46.a_ref = bf16[4,4096,256]{2,1,0:T(8,128)(2,1)S(1)} custom-call(s32[8,32]{1,0:T(8,128)S(1)} %bitcast.28, bf16[1024,4096]{1,0:T(8,128)(2,1)S(1)} %bitcast.22), custom_call_target="tpu_custom_call" | custom-call | flops 4194304 | bytes 16777216 | tf_op jit(solution)/shard_map/pallas_call | solution.py:75
  52.8 3.1 %shard_map.47 = (f32[128,1024]{1,0:T(8,128)S(1)}, f32[128,1024]{1,0:T(8,128)}) custom-call(s32[1]{0:T(128)} %bitcast.18.swap_ref, bf16[4,4096,256]{2,1,0:T(8,128)(2,1)S(1)} %shard_map.46.a_ref, bf16[64,4096]{1,0:T(8,128)(2,1)S(1)} %bitcast.27, bf16[64,4096]{1,0:T(8,128)(2,1)S(1)} %copy-done.10, bf16[64,4096]{1,0:T(8,128)(2,1)S(1)} %copy-done.12, ...), custom_call_target="tpu_custom_call" | custom-call | flops 2147483648 | bytes 11534336 | tf_op jit(solution)/shard_map/pallas_call | solution.py:108
  55.9 2.7 %collective-permute-done.6.refs_1_ = bf16[64,4096]{1,0:T(8,128)(2,1)} collective-permute-done((bf16[64,4096]{1,0:T(8,128)(2,1)}, bf16[64,4096]{1,0:T(8,128)(2,1)}, u32[]{:S(2)}, u32[]{:S(2)}) %collective-permute-start.6) | collective-permute-done | bytes 524320 | tf_op jit(solution)/shard_map/ppermute | solution.py:32
  58.9 3.0 %collective-permute-start.17 = (bf16[64,4096]{1,0:T(8,128)(2,1)}, bf16[64,4096]{1,0:T(8,128)(2,1)S(1)}, u32[]{:S(2)}, u32[]{:S(2)}) collective-permute-start(bf16[64,4096]{1,0:T(8,128)(2,1)} %collective-permute-done.14.refs_0_), channel_id=1, source_target_pairs={{0,48},{1,17},{2,50},{3,19},{4,52},{5,21},{6,54},{7,23},{8,56},{9,... | collective-permute-start | bytes 1572872 | tf_op jit(solution)/shard_map/ppermute | solution.py:32
  61.9 3.0 %collective-permute-start.15 = (bf16[64,4096]{1,0:T(8,128)(2,1)S(1)}, bf16[64,4096]{1,0:T(8,128)(2,1)S(1)}, u32[]{:S(2)}, u32[]{:S(2)}) collective-permute-start(bf16[64,4096]{1,0:T(8,128)(2,1)S(1)} %copy-done.10), channel_id=1, source_target_pairs={{0,192},{1,65},{2,194},{3,67},{4,196},{5,69},{6,198},{7,71},{8,200... | collective-permute-start | bytes 1572872 | tf_op jit(solution)/shard_map/ppermute | solution.py:32
  64.8 4.5 %shard_map.48 = (f32[128,1024]{1,0:T(8,128)S(1)}, f32[128,1024]{1,0:T(8,128)}) custom-call(s32[1]{0:T(128)} %bitcast.18.swap_ref, bf16[4,4096,256]{2,1,0:T(8,128)(2,1)S(1)} %shard_map.46.a_ref, bf16[64,4096]{1,0:T(8,128)(2,1)S(1)} %copy-done.7, bf16[64,4096]{1,0:T(8,128)(2,1)} %collective-permute-done.6.refs_1_, ...), custom_call_target="tpu_custom_call" | custom-call | flops 2147483648 | bytes 11534336 | tf_op jit(solution)/shard_map/pallas_call | solution.py:108
  69.3 2.2 %collective-permute-done.11.refs_1_ = bf16[64,4096]{1,0:T(8,128)(2,1)S(1)} collective-permute-done((bf16[64,4096]{1,0:T(8,128)(2,1)}, bf16[64,4096]{1,0:T(8,128)(2,1)S(1)}, u32[]{:S(2)}, u32[]{:S(2)}) %collective-permute-start.11) | collective-permute-done | bytes 524320 | tf_op jit(solution)/shard_map/ppermute | solution.py:32
  71.6 4.5 %shard_map.49 = (f32[128,1024]{1,0:T(8,128)S(1)}, f32[128,1024]{1,0:T(8,128)}) custom-call(s32[1]{0:T(128)} %bitcast.18.swap_ref, bf16[4,4096,256]{2,1,0:T(8,128)(2,1)S(1)} %shard_map.46.a_ref, bf16[64,4096]{1,0:T(8,128)(2,1)} %collective-permute-done.9.refs_0_, bf16[64,4096]{1,0:T(8,128)(2,1)S(1)} %collective-permute-done.11.refs_1_, ...), custom_call_target="tpu_custom_call" | custom-call | flops 2147483648 | bytes 11534336 | tf_op jit(solution)/shard_map/pallas_call | solution.py:108
  77.2 4.2 %shard_map.50 = (f32[128,1024]{1,0:T(8,128)S(1)}, f32[128,1024]{1,0:T(8,128)}) custom-call(s32[1]{0:T(128)} %bitcast.18.swap_ref, bf16[4,4096,256]{2,1,0:T(8,128)(2,1)S(1)} %shard_map.46.a_ref, bf16[64,4096]{1,0:T(8,128)(2,1)} %collective-permute-done.14.refs_0_, bf16[64,4096]{1,0:T(8,128)(2,1)S(1)} %collective-permute-done.15.refs_1_, ...), custom_call_target="tpu_custom_call" | custom-call | flops 2147483648 | bytes 11534336 | tf_op jit(solution)/shard_map/pallas_call | solution.py:108
  94.3 2.5 %collective-permute-start.23 = (bf16[64,1024]{1,0:T(8,128)(2,1)S(1)}, bf16[64,1024]{1,0:T(8,128)(2,1)S(1)}, u32[]{:S(2)}, u32[]{:S(2)}) collective-permute-start(bf16[64,1024]{1,0:T(8,128)(2,1)S(1)} %get-tuple-element.60), channel_id=1, source_target_pairs={{0,10},{1,11},{2,8},{3,9},{4,14},{5,15},{6,12},{7,13},{8,2},{9,3},... | collective-permute-start | bytes 393224 | tf_op jit(solution)/shard_map/ppermute | solution.py:48
  98.6 4.9 %collective-permute-done.20.refs_2_ = bf16[64,1024]{1,0:T(8,128)(2,1)S(1)} collective-permute-done((bf16[64,1024]{1,0:T(8,128)(2,1)S(1)}, bf16[64,1024]{1,0:T(8,128)(2,1)S(1)}, u32[]{:S(2)}, u32[]{:S(2)}) %collective-permute-start.20) | collective-permute-done | bytes 131104 | tf_op jit(solution)/shard_map/ppermute | solution.py:48
  105.1 4.3 %collective-permute-done.25.refs_7_ = bf16[64,1024]{1,0:T(8,128)(2,1)S(1)} collective-permute-done((bf16[64,1024]{1,0:T(8,128)(2,1)S(1)}, bf16[64,1024]{1,0:T(8,128)(2,1)S(1)}, u32[]{:S(2)}, u32[]{:S(2)}) %collective-permute-start.25) | collective-permute-done | bytes 131104 | tf_op jit(solution)/shard_map/ppermute | solution.py:48
  113.4 5.0 %collective-permute-done.26.b_ref = f32[4,64,128]{2,1,0:T(8,128)S(1)} collective-permute-done((f32[4,64,128]{2,1,0:T(8,128)S(1)}, f32[4,64,128]{2,1,0:T(8,128)S(1)}, u32[]{:S(2)}, u32[]{:S(2)}) %collective-permute-start.26) | collective-permute-done | bytes 131104 | tf_op jit(solution)/shard_map/ppermute | solution.py:22
  118.7 4.9 %collective-permute-start.29 = (f32[64,128]{1,0:T(8,128)S(1)}, f32[64,128]{1,0:T(8,128)S(1)}, u32[]{:S(2)}, u32[]{:S(2)}) collective-permute-start(f32[64,128]{1,0:T(8,128)S(1)} %get-tuple-element.68), channel_id=1, source_target_pairs={{0,64},{16,80},{32,96},{48,112},{64,128},{80,144},{96,160},{112,17... | collective-permute-start | bytes 98312 | tf_op jit(solution)/shard_map/ppermute | solution.py:22
  124.3 3.0 %collective-permute-start.31 = (f32[64,128]{1,0:T(8,128)S(1)}, f32[64,128]{1,0:T(8,128)S(1)}, u32[]{:S(2)}, u32[]{:S(2)}) collective-permute-start(f32[64,128]{1,0:T(8,128)S(1)} %get-tuple-element.70), channel_id=1, source_target_pairs={{0,192},{16,208},{32,224},{48,240},{64,0},{80,16},{96,32},{112,48}... | collective-permute-start | bytes 98312 | tf_op jit(solution)/shard_map/ppermute | solution.py:22
  127.3 4.1 %collective-permute-done.30.c_ref = f32[64,128]{1,0:T(8,128)S(1)} collective-permute-done((f32[64,128]{1,0:T(8,128)S(1)}, f32[64,128]{1,0:T(8,128)S(1)}, u32[]{:S(2)}, u32[]{:S(2)}) %collective-permute-start.30) | collective-permute-done | bytes 32800 | tf_op jit(solution)/shard_map/ppermute | solution.py:22
  (79 shorter events, 32.9 us)
Async XLA Ops:
  0.0 10.6 %collective-permute-start = (bf16[64,4096]{1,0:T(8,128)(2,1)}, bf16[64,4096]{1,0:T(8,128)(2,1)S(1)}, u32[]{:S(2)}, u32[]{:S(2)}) collective-permute-start(bf16[64,4096]{1,0:T(8,128)(2,1)} %bitcast.23), channel_id=1, source_target_pairs={{0,16},{1,49},{2,18},{3,51},{4,20},{5,53},{6,22},{7,55},{8,24},{9,... | collective-permute-start | bytes 1572872 | tf_op jit(solution)/shard_map/ppermute | solution.py:32
  1.5 15.7 %collective-permute-start.4 = (bf16[64,4096]{1,0:T(8,128)(2,1)}, bf16[64,4096]{1,0:T(8,128)(2,1)S(1)}, u32[]{:S(2)}, u32[]{:S(2)}) collective-permute-start(bf16[64,4096]{1,0:T(8,128)(2,1)} %bitcast.24), channel_id=1, source_target_pairs={{0,64},{1,193},{2,66},{3,195},{4,68},{5,197},{6,70},{7,199},{8,72}... | collective-permute-start | bytes 1572872 | tf_op jit(solution)/shard_map/ppermute | solution.py:32
  4.8 18.5 %collective-permute-start.2 = (bf16[64,4096]{1,0:T(8,128)(2,1)}, bf16[64,4096]{1,0:T(8,128)(2,1)S(1)}, u32[]{:S(2)}, u32[]{:S(2)}) collective-permute-start(bf16[64,4096]{1,0:T(8,128)(2,1)} %bitcast.25), channel_id=1, source_target_pairs={{0,48},{1,17},{2,50},{3,19},{4,52},{5,21},{6,54},{7,23},{8,56},{9,... | collective-permute-start | bytes 1572872 | tf_op jit(solution)/shard_map/ppermute | solution.py:32
  10.6 14.4 %collective-permute-start.1 = (bf16[64,4096]{1,0:T(8,128)(2,1)S(1)}, bf16[64,4096]{1,0:T(8,128)(2,1)S(1)}, u32[]{:S(2)}, u32[]{:S(2)}) collective-permute-start(bf16[64,4096]{1,0:T(8,128)(2,1)S(1)} %collective-permute-done.refs_2_), channel_id=1, source_target_pairs={{0,16},{1,49},{2,18},{3,51},{4,20},{5,53},{6,22},{7,55},{8,24},{9,... | collective-permute-start | bytes 1572872 | tf_op jit(solution)/shard_map/ppermute | solution.py:32
  17.1 19.5 %collective-permute-start.9 = (bf16[64,4096]{1,0:T(8,128)(2,1)S(1)}, bf16[64,4096]{1,0:T(8,128)(2,1)}, u32[]{:S(2)}, u32[]{:S(2)}) collective-permute-start(bf16[64,4096]{1,0:T(8,128)(2,1)S(1)} %collective-permute-done.4.refs_0_), channel_id=1, source_target_pairs={{0,64},{1,193},{2,66},{3,195},{4,68},{5,197},{6,70},{7,199},{8,72}... | collective-permute-start | bytes 1572872 | tf_op jit(solution)/shard_map/ppermute | solution.py:32
  21.8 16.4 %collective-permute-start.5 = (bf16[64,4096]{1,0:T(8,128)(2,1)S(1)}, bf16[64,4096]{1,0:T(8,128)(2,1)}, u32[]{:S(2)}, u32[]{:S(2)}) collective-permute-start(bf16[64,4096]{1,0:T(8,128)(2,1)S(1)} %collective-permute-done.4.refs_0_), channel_id=1, source_target_pairs={{0,16},{1,49},{2,18},{3,51},{4,20},{5,53},{6,22},{7,55},{8,24},{9,... | collective-permute-start | bytes 1572872 | tf_op jit(solution)/shard_map/ppermute | solution.py:32
  23.3 32.6 %collective-permute-start.7 = (bf16[64,4096]{1,0:T(8,128)(2,1)S(1)}, bf16[64,4096]{1,0:T(8,128)(2,1)}, u32[]{:S(2)}, u32[]{:S(2)}) collective-permute-start(bf16[64,4096]{1,0:T(8,128)(2,1)S(1)} %collective-permute-done.4.refs_0_), channel_id=1, source_target_pairs={{0,48},{1,17},{2,50},{3,19},{4,52},{5,21},{6,54},{7,23},{8,56},{9,... | collective-permute-start | bytes 1572872 | tf_op jit(solution)/shard_map/ppermute | solution.py:32
  36.7 19.2 %collective-permute-start.10 = (bf16[64,4096]{1,0:T(8,128)(2,1)}, bf16[64,4096]{1,0:T(8,128)(2,1)}, u32[]{:S(2)}, u32[]{:S(2)}) collective-permute-start(bf16[64,4096]{1,0:T(8,128)(2,1)} %collective-permute-done.9.refs_0_), channel_id=1, source_target_pairs={{0,16},{1,49},{2,18},{3,51},{4,20},{5,53},{6,22},{7,55},{8,24},{9,... | collective-permute-start | bytes 1572872 | tf_op jit(solution)/shard_map/ppermute | solution.py:32
  38.2 20.4 %collective-permute-start.6 = (bf16[64,4096]{1,0:T(8,128)(2,1)}, bf16[64,4096]{1,0:T(8,128)(2,1)}, u32[]{:S(2)}, u32[]{:S(2)}) collective-permute-start(bf16[64,4096]{1,0:T(8,128)(2,1)} %collective-permute-done.5.refs_2_), channel_id=1, source_target_pairs={{0,16},{1,49},{2,18},{3,51},{4,20},{5,53},{6,22},{7,55},{8,24},{9,... | collective-permute-start | bytes 1572872 | tf_op jit(solution)/shard_map/ppermute | solution.py:32
  39.3 19.6 %collective-permute-start.12 = (bf16[64,4096]{1,0:T(8,128)(2,1)}, bf16[64,4096]{1,0:T(8,128)(2,1)}, u32[]{:S(2)}, u32[]{:S(2)}) collective-permute-start(bf16[64,4096]{1,0:T(8,128)(2,1)} %collective-permute-done.9.refs_0_), channel_id=1, source_target_pairs={{0,48},{1,17},{2,50},{3,19},{4,52},{5,21},{6,54},{7,23},{8,56},{9,... | collective-permute-start | bytes 1572872 | tf_op jit(solution)/shard_map/ppermute | solution.py:32
  41.4 17.5 %collective-permute-start.14 = (bf16[64,4096]{1,0:T(8,128)(2,1)}, bf16[64,4096]{1,0:T(8,128)(2,1)}, u32[]{:S(2)}, u32[]{:S(2)}) collective-permute-start(bf16[64,4096]{1,0:T(8,128)(2,1)} %bitcast.26), channel_id=1, source_target_pairs={{0,192},{1,65},{2,194},{3,67},{4,196},{5,69},{6,198},{7,71},{8,200... | collective-permute-start | bytes 1572872 | tf_op jit(solution)/shard_map/ppermute | solution.py:32
  58.6 12.9 %collective-permute-start.11 = (bf16[64,4096]{1,0:T(8,128)(2,1)}, bf16[64,4096]{1,0:T(8,128)(2,1)S(1)}, u32[]{:S(2)}, u32[]{:S(2)}) collective-permute-start(bf16[64,4096]{1,0:T(8,128)(2,1)} %collective-permute-done.10.refs_2_), channel_id=1, source_target_pairs={{0,16},{1,49},{2,18},{3,51},{4,20},{5,53},{6,22},{7,55},{8,24},{9,... | collective-permute-start | bytes 1572872 | tf_op jit(solution)/shard_map/ppermute | solution.py:32
  58.9 17.2 %collective-permute-start.17 = (bf16[64,4096]{1,0:T(8,128)(2,1)}, bf16[64,4096]{1,0:T(8,128)(2,1)S(1)}, u32[]{:S(2)}, u32[]{:S(2)}) collective-permute-start(bf16[64,4096]{1,0:T(8,128)(2,1)} %collective-permute-done.14.refs_0_), channel_id=1, source_target_pairs={{0,48},{1,17},{2,50},{3,19},{4,52},{5,21},{6,54},{7,23},{8,56},{9,... | collective-permute-start | bytes 1572872 | tf_op jit(solution)/shard_map/ppermute | solution.py:32
  61.9 15.3 %collective-permute-start.16 = (bf16[64,4096]{1,0:T(8,128)(2,1)}, bf16[64,4096]{1,0:T(8,128)(2,1)S(1)}, u32[]{:S(2)}, u32[]{:S(2)}) collective-permute-start(bf16[64,4096]{1,0:T(8,128)(2,1)} %collective-permute-done.14.refs_0_), channel_id=1, source_target_pairs={{0,16},{1,49},{2,18},{3,51},{4,20},{5,53},{6,22},{7,55},{8,24},{9,... | collective-permute-start | bytes 1572872 | tf_op jit(solution)/shard_map/ppermute | solution.py:32
  61.9 15.3 %collective-permute-start.15 = (bf16[64,4096]{1,0:T(8,128)(2,1)S(1)}, bf16[64,4096]{1,0:T(8,128)(2,1)S(1)}, u32[]{:S(2)}, u32[]{:S(2)}) collective-permute-start(bf16[64,4096]{1,0:T(8,128)(2,1)S(1)} %copy-done.10), channel_id=1, source_target_pairs={{0,192},{1,65},{2,194},{3,67},{4,196},{5,69},{6,198},{7,71},{8,200... | collective-permute-start | bytes 1572872 | tf_op jit(solution)/shard_map/ppermute | solution.py:32
  64.8 20.1 %collective-permute-start.3 = (f32[128,1024]{1,0:T(8,128)}, f32[128,1024]{1,0:T(8,128)}, u32[]{:S(2)}, u32[]{:S(2)}) collective-permute-start(f32[128,1024]{1,0:T(8,128)} %get-tuple-element.39.refs_5_), channel_id=1, source_target_pairs={{0,1},{1,0},{2,3},{3,2},{4,5},{5,4},{6,7},{7,6},{8,9},{9,8},{10,11... | collective-permute-start | bytes 1572872 | tf_op jit(solution)/shard_map/ppermute | solution.py:52
  71.6 13.4 %collective-permute-start.8 = (f32[128,1024]{1,0:T(8,128)}, f32[128,1024]{1,0:T(8,128)}, u32[]{:S(2)}, u32[]{:S(2)}) collective-permute-start(f32[128,1024]{1,0:T(8,128)} %get-tuple-element.43.refs_5_), channel_id=1, source_target_pairs={{0,1},{1,0},{2,3},{3,2},{4,5},{5,4},{6,7},{7,6},{8,9},{9,8},{10,11... | collective-permute-start | bytes 1572872 | tf_op jit(solution)/shard_map/ppermute | solution.py:52
  90.9 12.6 %collective-permute-start.20 = (bf16[64,1024]{1,0:T(8,128)(2,1)S(1)}, bf16[64,1024]{1,0:T(8,128)(2,1)S(1)}, u32[]{:S(2)}, u32[]{:S(2)}) collective-permute-start(bf16[64,1024]{1,0:T(8,128)(2,1)S(1)} %get-tuple-element.57), channel_id=1, source_target_pairs={{0,4},{1,13},{2,6},{3,15},{4,8},{5,1},{6,10},{7,3},{8,12},{9,5},{1... | collective-permute-start | bytes 393224 | tf_op jit(solution)/shard_map/ppermute | solution.py:48
  92.2 11.4 %collective-permute-start.21 = (bf16[64,1024]{1,0:T(8,128)(2,1)S(1)}, bf16[64,1024]{1,0:T(8,128)(2,1)S(1)}, u32[]{:S(2)}, u32[]{:S(2)}) collective-permute-start(bf16[64,1024]{1,0:T(8,128)(2,1)S(1)} %get-tuple-element.58), channel_id=1, source_target_pairs={{0,6},{1,15},{2,4},{3,13},{4,10},{5,3},{6,8},{7,1},{8,14},{9,7},{1... | collective-permute-start | bytes 393224 | tf_op jit(solution)/shard_map/ppermute | solution.py:48
  92.3 12.7 %collective-permute-start.22 = (bf16[64,1024]{1,0:T(8,128)(2,1)S(1)}, bf16[64,1024]{1,0:T(8,128)(2,1)S(1)}, u32[]{:S(2)}, u32[]{:S(2)}) collective-permute-start(bf16[64,1024]{1,0:T(8,128)(2,1)S(1)} %get-tuple-element.59), channel_id=1, source_target_pairs={{0,8},{1,9},{2,10},{3,11},{4,12},{5,13},{6,14},{7,15},{8,0},{9,1},... | collective-permute-start | bytes 393224 | tf_op jit(solution)/shard_map/ppermute | solution.py:48
  94.3 10.7 %collective-permute-start.23 = (bf16[64,1024]{1,0:T(8,128)(2,1)S(1)}, bf16[64,1024]{1,0:T(8,128)(2,1)S(1)}, u32[]{:S(2)}, u32[]{:S(2)}) collective-permute-start(bf16[64,1024]{1,0:T(8,128)(2,1)S(1)} %get-tuple-element.60), channel_id=1, source_target_pairs={{0,10},{1,11},{2,8},{3,9},{4,14},{5,15},{6,12},{7,13},{8,2},{9,3},... | collective-permute-start | bytes 393224 | tf_op jit(solution)/shard_map/ppermute | solution.py:48
  96.8 8.2 %collective-permute-start.24 = (bf16[64,1024]{1,0:T(8,128)(2,1)S(1)}, bf16[64,1024]{1,0:T(8,128)(2,1)S(1)}, u32[]{:S(2)}, u32[]{:S(2)}) collective-permute-start(bf16[64,1024]{1,0:T(8,128)(2,1)S(1)} %get-tuple-element.61), channel_id=1, source_target_pairs={{0,12},{1,5},{2,14},{3,7},{4,0},{5,9},{6,2},{7,11},{8,4},{9,13},{1... | collective-permute-start | bytes 393224 | tf_op jit(solution)/shard_map/ppermute | solution.py:48
  110.1 8.3 %collective-permute-start.26 = (f32[4,64,128]{2,1,0:T(8,128)S(1)}, f32[4,64,128]{2,1,0:T(8,128)S(1)}, u32[]{:S(2)}, u32[]{:S(2)}) collective-permute-start(f32[4,64,128]{2,1,0:T(8,128)S(1)} %get-tuple-element.64), channel_id=1, source_target_pairs={{0,16},{16,32},{32,48},{48,0},{64,80},{80,96},{96,112},{112,64},{1... | collective-permute-start | bytes 393224 | tf_op jit(solution)/shard_map/ppermute | solution.py:22
  118.7 8.6 %collective-permute-start.29 = (f32[64,128]{1,0:T(8,128)S(1)}, f32[64,128]{1,0:T(8,128)S(1)}, u32[]{:S(2)}, u32[]{:S(2)}) collective-permute-start(f32[64,128]{1,0:T(8,128)S(1)} %get-tuple-element.68), channel_id=1, source_target_pairs={{0,64},{16,80},{32,96},{48,112},{64,128},{80,144},{96,160},{112,17... | collective-permute-start | bytes 98312 | tf_op jit(solution)/shard_map/ppermute | solution.py:22
  (22 other events, 136.8 us)
